TPU v7x, 32 devices: a whole 2x2x4 slice. The times are simulated.
32 devices in a mesh: band: 4 (over z), mem: 8 (over y, x, core).
Axes of the slice: x: 2, y: 2, z: 4, core: 2. Of those that a mesh axis runs over, the one named last changes fastest.
Arguments:
- prior_ensemble: bfloat16 [1024, 65536], P('mem', 'band'), may hold values from -6 to 6
- perturbed_measurements: bfloat16 [1024, 4096], P('mem', 'band'), may hold values from -6 to 6
- solved_residuals: bfloat16 [1024, 4096], P('mem', 'band'), may hold values from -6 to 6
- localisation_matrix: float32 [8, 128, 128], replicated, may hold values from 0 to 1
- piece_owner_device: int32 [512], P('band'), may hold values from 0 to 7, as said below
- measurement_group_matrix: int32 [512, 6], P('band'), may hold values from 0 to 31, as said below
- localisation_factors: int32 [512, 6], P('band'), may hold values from 0 to 7
Outputs:
- analysis: bfloat16 [1024, 65536], P('mem', 'band')
- spread: float32 [1024, 128], P(('band', 'mem'))
Inputs may be any that keep to these rules, and one draw needn't show every extreme that they name: `piece_owner_device`: within a band, no owner has more than 32 patches, and in every band one owner has exactly 32. `measurement_group_matrix`: patch p of band b = p // 128 has the centre block c = b * 8 + (p - b * 128) // 16 and uses only blocks c - 2 to c + 2.
All inputs are finite; a program needn't handle non-finite values.
Results may differ from a plain program's by a relative error of at most 0.0065.
Values may be sent and summed in bfloat16 or wider, within the bound.
No kernel may reach another device: no remote copies, remote signals or barrier semaphores. Data moves between devices by JAX's collectives and lax.ppermute only.
A program may use at most 192 MiB of HBM per device.

v0:
```python
import functools

import jax
import jax.numpy as jnp
from jax import lax
from jax.experimental import pallas as pl
from jax.experimental.pallas import tpu as pltpu
from jax.sharding import PartitionSpec as P

RIM_BLOCKS = 2
CHUNKS = 2
STEP_PATCHES = 2
PAD_ROWS = 16
VMEM_BYTES = 48 * 1024 * 1024


def prepare_kernel(count, rows, width, obs_len, place_ref, *refs):
    pieces, (ydt_ref, solved_ref, ysum_ref) = refs[:count], refs[count:]
    offset = pl.multiple_of(place_ref[0] * obs_len, obs_len)
    window = pl.ds(offset, width)
    members = count * rows
    total = jnp.zeros((1, width), jnp.float32)
    for piece in pieces:
        total = total + jnp.sum(piece[0, :, window].astype(jnp.float32), axis=0, keepdims=True)
    centre = total / members
    for i, piece in enumerate(pieces):
        place = slice(i * rows, (i + 1) * rows)
        dev = piece[0, :, window].astype(jnp.float32) - centre
        ydt_ref[:width, place] = jnp.transpose(dev).astype(jnp.bfloat16)
        solved_ref[place, :] = piece[1, :, window]
    ydt_ref[width:, :] = jnp.ones((ydt_ref.shape[0] - width, members), jnp.bfloat16)
    ysum_ref[...] = jnp.dot(
        ydt_ref[:width, :],
        jnp.ones((members, ysum_ref.shape[1]), jnp.bfloat16),
        preferred_element_type=jnp.float32,
    )


def analyse_kernel(count, rows, span, obs_len, nblk, block_ref, taper_ref, *refs):
    priors, (ydt_ref, solved_ref, ysum_ref, loc_ref) = refs[:count], refs[count : count + 4]
    outs, (var_ref, weight_ref) = refs[count + 4 : 2 * count + 4], refs[2 * count + 4 :]
    step = pl.program_id(0)
    width = solved_ref.shape[1]
    members = count * rows
    patches = priors[0].shape[1] // span
    weight_ref[...] = jnp.zeros_like(weight_ref)
    for j in range(patches):
        for k in range(nblk):
            at = (step * patches + j) * nblk + k
            row = pl.multiple_of(block_ref[at] * obs_len, obs_len)
            there = (pl.ds(row, obs_len), slice(j * span, (j + 1) * span))
            weight_ref[there] = weight_ref[there] + loc_ref[taper_ref[at]]
    prior = jnp.concatenate([ref[...] for ref in priors], axis=0)
    product = jnp.dot(ydt_ref[...], prior, preferred_element_type=jnp.float32)
    mean = product[width : width + 1, :] * (1.0 / members)
    ysum = jnp.concatenate([ysum_ref[...]] * patches, axis=1)
    cov = product[:width, :] - ysum * mean
    tapered = (cov * weight_ref[...]).astype(jnp.bfloat16)
    increment = jnp.dot(solved_ref[...], tapered, preferred_element_type=jnp.float32)
    updated = (prior.astype(jnp.float32) + increment).astype(jnp.bfloat16)
    for i, out in enumerate(outs):
        out[...] = updated[i * rows : (i + 1) * rows, :]
    updated = updated.astype(jnp.float32)
    centre = jnp.sum(updated, axis=0, keepdims=True) * (1.0 / members)
    variance = jnp.sum((updated - centre) ** 2, axis=0, keepdims=True) * (1.0 / members)
    for j in range(patches):
        var_ref[pl.ds(step * patches + j, 1), :] = variance[:, j * span : (j + 1) * span]


def spread_kernel(per_worker, owner_ref, place_ref, var_ref, out_ref):
    me = place_ref[0]
    out_ref[...] = jnp.zeros_like(out_ref)

    def one(patch, filled):
        mine = owner_ref[patch] == me
        relative = jnp.bitwise_xor(patch // per_worker, me)

        @pl.when(mine)
        def _():
            source = relative * per_worker + patch % per_worker
            out_ref[pl.ds(filled, 1), :] = var_ref[pl.ds(source, 1), :]

        return filled + mine.astype(jnp.int32)

    lax.fori_loop(0, owner_ref.shape[0], one, jnp.int32(0))


def whole(shape):
    return pl.BlockSpec(shape, lambda *_: (0,) * len(shape))


def per_device(
    prior_ensemble,
    perturbed_measurements,
    solved_residuals,
    localisation_matrix,
    piece_owner_device,
    measurement_group_matrix,
    localisation_factors,
):
    rows, vector_span = prior_ensemble.shape
    taper_count, span, obs_len = localisation_matrix.shape
    nblk = measurement_group_matrix.shape[1]
    count, bands = lax.axis_size("mem"), lax.axis_size("band")
    members = rows * count
    strip = vector_span // span
    band_blocks = perturbed_measurements.shape[1] // obs_len
    per_worker = strip // count
    centres = per_worker * band_blocks // strip
    assert centres * strip == per_worker * band_blocks and count & (count - 1) == 0
    window = 2 * RIM_BLOCKS + centres
    width = window * obs_len
    strip_position = lax.axis_index("band")
    me = lax.axis_index("mem")

    def partner(x, flip):
        return lax.ppermute(x, "mem", [(i, i ^ flip) for i in range(count)])

    both = jnp.stack([perturbed_measurements, solved_residuals])
    up = [(i, i + 1) for i in range(bands - 1)]
    down = [(j, i) for i, j in up]
    rim = RIM_BLOCKS * obs_len
    before = lax.ppermute(both[:, :, -rim:], "band", up)
    after = lax.ppermute(both[:, :, :rim], "band", down)
    padded = jnp.concatenate([before, both, after], axis=2)
    pair_width = (window + centres) * obs_len

    def pair_window(flip):
        first = ((me ^ flip) >> 1) * (2 * centres * obs_len)
        return lax.dynamic_slice_in_dim(padded, first, pair_width, 2)

    chunk_patches = per_worker // CHUNKS
    chunk_span = chunk_patches * span

    def outgoing(flip, chunk):
        first = (me ^ flip) * (per_worker * span) + chunk * chunk_span
        return lax.dynamic_slice_in_dim(prior_ensemble, first, chunk_span, 1)

    order = list(range(2, count, 2)) + list(range(3, count, 2)) + [1]

    def scatter_prior(chunk):
        got = {0: outgoing(0, chunk)}
        for flip in order:
            got[flip] = partner(outgoing(flip, chunk), flip)
        return [got[i] for i in range(count)]

    priors = [scatter_prior(0)]
    even = {0: pair_window(0)}
    for flip in range(2, count, 2):
        even[flip] = partner(pair_window(flip), flip)
    pieces = []
    for flip in range(0, count, 2):
        pieces += [even[flip], partner(even[flip], 1)]
    for chunk in range(1, CHUNKS):
        priors.append(scatter_prior(chunk))

    parity = jnp.reshape((me & 1) * centres, (1,)).astype(jnp.int32)
    ydt, solved, ysum = pl.pallas_call(
        functools.partial(prepare_kernel, count, rows, width, obs_len),
        grid_spec=pltpu.PrefetchScalarGridSpec(
            num_scalar_prefetch=1,
            grid=(1,),
            in_specs=[whole((2, rows, pair_width))] * count,
            out_specs=[
                whole((width + PAD_ROWS, members)),
                whole((members, width)),
                whole((width, span)),
            ],
        ),
        out_shape=[
            jax.ShapeDtypeStruct((width + PAD_ROWS, members), jnp.bfloat16),
            jax.ShapeDtypeStruct((members, width), jnp.bfloat16),
            jax.ShapeDtypeStruct((width, span), jnp.float32),
        ],
        compiler_params=pltpu.CompilerParams(vmem_limit_bytes=VMEM_BYTES),
        cost_estimate=pl.CostEstimate(
            flops=20 * members * width, bytes_accessed=8 * members * width, transcendentals=0
        ),
    )(parity, *pieces)

    taper = jnp.transpose(localisation_matrix, (0, 2, 1)) * (1.0 / (members - 1))
    first_block = strip_position * band_blocks + me * centres - RIM_BLOCKS
    start = me * per_worker
    blocks = lax.dynamic_slice_in_dim(measurement_group_matrix, start, per_worker, 0) - first_block
    tapers = lax.dynamic_slice_in_dim(localisation_factors, start, per_worker, 0)

    step_span = STEP_PATCHES * span
    piece_spec = pl.BlockSpec((rows, step_span), lambda i, *_: (0, i))

    def analyse(chunk, prior):
        mine = slice(chunk * chunk_patches, (chunk + 1) * chunk_patches)
        *out, variance = pl.pallas_call(
            functools.partial(analyse_kernel, count, rows, span, obs_len, nblk),
            grid_spec=pltpu.PrefetchScalarGridSpec(
                num_scalar_prefetch=2,
                grid=(chunk_patches // STEP_PATCHES,),
                in_specs=[piece_spec] * count
                + [
                    whole((width + PAD_ROWS, members)),
                    whole((members, width)),
                    whole((width, span)),
                    whole((taper_count, obs_len, span)),
                ],
                out_specs=[piece_spec] * count + [whole((chunk_patches, span))],
                scratch_shapes=[pltpu.VMEM((width, step_span), jnp.float32)],
            ),
            out_shape=[jax.ShapeDtypeStruct((rows, chunk_span), jnp.bfloat16)] * count
            + [jax.ShapeDtypeStruct((chunk_patches, span), jnp.float32)],
            compiler_params=pltpu.CompilerParams(vmem_limit_bytes=VMEM_BYTES),
            cost_estimate=pl.CostEstimate(
                flops=4 * members * width * chunk_span,
                bytes_accessed=4 * members * (width + chunk_span),
                transcendentals=0,
            ),
        )(blocks[mine].reshape(-1), tapers[mine].reshape(-1), *prior, ydt, solved, ysum, taper)
        return out, variance

    analysis = jnp.zeros(prior_ensemble.shape, prior_ensemble.dtype)
    variances = []
    for chunk in range(CHUNKS):
        out, variance = analyse(chunk, priors[chunk])
        variances.append(variance)
        for flip in order + [0]:
            piece = partner(out[flip], flip) if flip else out[0]
            first = (me ^ flip) * (per_worker * span) + chunk * chunk_span
            analysis = lax.dynamic_update_slice(analysis, piece, (0, first))

    gathered = jnp.concatenate(variances, axis=0)
    flip = 1
    while flip < count:
        gathered = jnp.concatenate([gathered, partner(gathered, flip)], axis=0)
        flip *= 2
    spread = pl.pallas_call(
        functools.partial(spread_kernel, per_worker),
        grid_spec=pltpu.PrefetchScalarGridSpec(
            num_scalar_prefetch=2,
            grid=(1,),
            in_specs=[whole((strip, span))],
            out_specs=whole((2 * per_worker, span)),
        ),
        out_shape=jax.ShapeDtypeStruct((2 * per_worker, span), jnp.float32),
    )(piece_owner_device, jnp.reshape(me, (1,)).astype(jnp.int32), gathered)
    return analysis, spread


def solution(mesh):
    return jax.shard_map(
        per_device,
        mesh=mesh,
        in_specs=(
            P("mem", "band"),
            P("mem", "band"),
            P("mem", "band"),
            P(),
            P("band"),
            P("band", None),
            P("band", None),
        ),
        out_specs=(P("mem", "band"), P(("band", "mem"), None)),
        check_vma=False,
    )
```

profile of v0, /device:TPU:0, one launch (start us, length us, event | category | flops | bytes accessed | tf_op | source)
XLA Modules:
  0.0 175.8 jit_solution(12033854169651063848)
XLA Ops:
  1.6 4.9 %collective-permute-start.7 = (bf16[2,128,256]{2,1,0:T(8,128)(2,1)S(1)}, bf16[2,128,256]{2,1,0:T(8,128)(2,1)S(1)}, u32[]{:S(2)}, u32[]{:S(2)}) collective-permute-start(bf16[2,128,256]{2,1,0:T(8,128)(2,1)S(1)} %get-tuple-element.64), channel_id=1, source_target_pairs={{0,8},{8,16},{16,24},{1,9},{9,17},{17,25},{2,10},{10,18},{18,26},{... | collective-permute-start | bytes 393224 | tf_op jit(solution)/shard_map/ppermute | solution.py:123
  7.9 4.0 %constant_dynamic-slice_fusion = (bf16[128,1024]{1,0:T(8,128)(2,1)}, bf16[128,1024]{1,0:T(8,128)(2,1)}, bf16[128,1024]{1,0:T(8,128)(2,1)}, bf16[128,1024]{1,0:T(...) fusion(bf16[128,16384]{1,0:T(8,128)(2,1)} %param.7, ...), kind=kLoop, calls=%fused_computation.19 | loop fusion | bytes 8388672 | tf_op jit(solution)/shard_map/dynamic_slice | solution.py:137
  13.6 1.6 collective-permute-start.10
  19.3 18.6 %collective-permute-done.24.refs_2_ = bf16[128,1024]{1,0:T(8,128)(2,1)S(1)} collective-permute-done((bf16[128,1024]{1,0:T(8,128)(2,1)S(1)}, bf16[128,1024]{1,0:T(8,128)(2,1)S(1)}, u32[]{:S(2)}, u32[]{:S(2)}) %collective-permute-start.24) | collective-permute-done | bytes 262176 | tf_op jit(solution)/shard_map/ppermute | solution.py:117
  41.3 6.8 %collective-permute-done.1.refs_2_ = bf16[128,1024]{1,0:T(8,128)(2,1)S(1)} collective-permute-done((bf16[128,1024]{1,0:T(8,128)(2,1)}, bf16[128,1024]{1,0:T(8,128)(2,1)S(1)}, u32[]{:S(2)}, u32[]{:S(2)}) %collective-permute-start.1) | collective-permute-done | bytes 262176 | tf_op jit(solution)/shard_map/ppermute | solution.py:117
  54.4 2.0 %copy.11 = f32[8,128,128]{1,2,0:T(8,128)} copy(f32[8,128,128]{2,1,0:T(8,128)} %param.10) | data formatting | bytes 1048576 | tf_op args[3]
  62.3 6.2 %collective-permute-done.3.refs_4_ = bf16[128,1024]{1,0:T(8,128)(2,1)} collective-permute-done((bf16[128,1024]{1,0:T(8,128)(2,1)}, bf16[128,1024]{1,0:T(8,128)(2,1)}, u32[]{:S(2)}, u32[]{:S(2)}) %collective-permute-start.3) | collective-permute-done | bytes 262176 | tf_op jit(solution)/shard_map/ppermute | solution.py:117
  68.5 2.6 %collective-permute-start.26 = (bf16[128,1024]{1,0:T(8,128)(2,1)S(1)}, bf16[128,1024]{1,0:T(8,128)(2,1)S(1)}, u32[]{:S(2)}, u32[]{:S(2)}) collective-permute-start(bf16[128,1024]{1,0:T(8,128)(2,1)S(1)} %copy-done.15), channel_id=1, source_target_pairs={{0,4},{1,5},{2,6},{3,7},{4,0},{5,1},{6,2},{7,3},{8,12},{9,13},{10,... | collective-permute-start | bytes 786440 | tf_op jit(solution)/shard_map/ppermute | solution.py:117
  71.1 4.8 %collective-permute-done.4.refs_5_ = bf16[128,1024]{1,0:T(8,128)(2,1)} collective-permute-done((bf16[128,1024]{1,0:T(8,128)(2,1)}, bf16[128,1024]{1,0:T(8,128)(2,1)}, u32[]{:S(2)}, u32[]{:S(2)}) %collective-permute-start.4) | collective-permute-done | bytes 262176 | tf_op jit(solution)/shard_map/ppermute | solution.py:117
  77.6 2.1 %collective-permute-start.29 = (bf16[128,1024]{1,0:T(8,128)(2,1)S(1)}, bf16[128,1024]{1,0:T(8,128)(2,1)S(1)}, u32[]{:S(2)}, u32[]{:S(2)}) collective-permute-start(bf16[128,1024]{1,0:T(8,128)(2,1)S(1)} %copy-done.12), channel_id=1, source_target_pairs={{0,7},{1,6},{2,5},{3,4},{4,3},{5,2},{6,1},{7,0},{8,15},{9,14},{10,... | collective-permute-start | bytes 786440 | tf_op jit(solution)/shard_map/ppermute | solution.py:117
  79.7 12.0 %shard_map.87 = (bf16[128,1024]{1,0:T(8,128)(2,1)S(1)}, bf16[128,1024]{1,0:T(8,128)(2,1)S(1)}, bf16[128,1024]{1,0:T(8,128)(2,1)}, bf16[128,1024]{1,0:T(8,128)(2,...) custom-call(s32[48]{0:T(128)S(1)} %reshape.22.block_ref, ...), custom_call_target="tpu_custom_call" | custom-call | flops 2684354560 | bytes 6815744 | tf_op jit(solution)/shard_map/pallas_call | solution.py:192
  91.8 6.1 %collective-permute-done.27.refs_5_ = bf16[128,1024]{1,0:T(8,128)(2,1)S(1)} collective-permute-done((bf16[128,1024]{1,0:T(8,128)(2,1)S(1)}, bf16[128,1024]{1,0:T(8,128)(2,1)S(1)}, u32[]{:S(2)}, u32[]{:S(2)}) %collective-permute-start.27) | collective-permute-done | bytes 262176 | tf_op jit(solution)/shard_map/ppermute | solution.py:117
  97.9 11.4 %shard_map.88 = (bf16[128,1024]{1,0:T(8,128)(2,1)S(1)}, bf16[128,1024]{1,0:T(8,128)(2,1)S(1)}, bf16[128,1024]{1,0:T(8,128)(2,1)S(1)}, bf16[128,1024]{1,0:T(8,128...) custom-call(s32[48]{0:T(128)S(1)} %reshape.25.block_ref, ...), custom_call_target="tpu_custom_call" | custom-call | flops 2684354560 | bytes 6815744 | tf_op jit(solution)/shard_map/pallas_call | solution.py:192
  115.0 14.7 %collective-permute-done.38 = f32[32,128]{1,0:T(8,128)S(1)} collective-permute-done((f32[32,128]{1,0:T(8,128)S(1)}, f32[32,128]{1,0:T(8,128)S(1)}, u32[]{:S(2)}, u32[]{:S(2)}) %collective-permute-start.38) | collective-permute-done | bytes 16416 | tf_op jit(solution)/shard_map/ppermute | solution.py:117
  131.2 2.4 %collective-permute-done.39 = f32[64,128]{1,0:T(8,128)S(1)} collective-permute-done((f32[64,128]{1,0:T(8,128)S(1)}, f32[64,128]{1,0:T(8,128)S(1)}, u32[]{:S(2)}, u32[]{:S(2)}) %collective-permute-start.39) | collective-permute-done | bytes 32800 | tf_op jit(solution)/shard_map/ppermute | solution.py:117
  134.3 3.3 %shard_map.89 = f32[32,128]{1,0:T(8,128)} custom-call(s32[128]{0:T(128)} %owner_ref.1, s32[1]{0:T(128)} %bitcast.4.place_ref, f32[128,128]{1,0:T(8,128)} %copy-done.17), custom_call_target="tpu_custom_call" | custom-call | tf_op jit(solution)/shard_map/pallas_call | solution.py:233
  137.6 2.1 %collective-permute-start.20 = (bf16[128,1024]{1,0:T(8,128)(2,1)S(1)}, bf16[128,1024]{1,0:T(8,128)(2,1)S(1)}, u32[]{:S(2)}, u32[]{:S(2)}) collective-permute-start(bf16[128,1024]{1,0:T(8,128)(2,1)S(1)} %get-tuple-element.30), channel_id=1, source_target_pairs={{0,5},{1,4},{2,7},{3,6},{4,1},{5,0},{6,3},{7,2},{8,13},{9,12},{10,... | collective-permute-start | bytes 786440 | tf_op jit(solution)/shard_map/ppermute | solution.py:117
  146.9 5.1 %collective-permute-done.20 = bf16[128,1024]{1,0:T(8,128)(2,1)S(1)} collective-permute-done((bf16[128,1024]{1,0:T(8,128)(2,1)S(1)}, bf16[128,1024]{1,0:T(8,128)(2,1)S(1)}, u32[]{:S(2)}, u32[]{:S(2)}) %collective-permute-start.20) | collective-permute-done | bytes 262176 | tf_op jit(solution)/shard_map/ppermute | solution.py:117
  153.2 2.1 %collective-permute-start.33 = (bf16[128,1024]{1,0:T(8,128)(2,1)S(1)}, bf16[128,1024]{1,0:T(8,128)(2,1)S(1)}, u32[]{:S(2)}, u32[]{:S(2)}) collective-permute-start(bf16[128,1024]{1,0:T(8,128)(2,1)S(1)} %get-tuple-element.37), channel_id=1, source_target_pairs={{0,3},{1,2},{2,1},{3,0},{4,7},{5,6},{6,5},{7,4},{8,11},{9,10},{10,... | collective-permute-start | bytes 786440 | tf_op jit(solution)/shard_map/ppermute | solution.py:117
  155.5 2.0 %collective-permute-start.35 = (bf16[128,1024]{1,0:T(8,128)(2,1)S(1)}, bf16[128,1024]{1,0:T(8,128)(2,1)S(1)}, u32[]{:S(2)}, u32[]{:S(2)}) collective-permute-start(bf16[128,1024]{1,0:T(8,128)(2,1)S(1)} %get-tuple-element.39), channel_id=1, source_target_pairs={{0,7},{1,6},{2,5},{3,4},{4,3},{5,2},{6,1},{7,0},{8,15},{9,14},{10,... | collective-permute-start | bytes 786440 | tf_op jit(solution)/shard_map/ppermute | solution.py:117
  157.5 6.8 %collective-permute-done.31 = bf16[128,1024]{1,0:T(8,128)(2,1)S(1)} collective-permute-done((bf16[128,1024]{1,0:T(8,128)(2,1)S(1)}, bf16[128,1024]{1,0:T(8,128)(2,1)S(1)}, u32[]{:S(2)}, u32[]{:S(2)}) %collective-permute-start.31) | collective-permute-done | bytes 262176 | tf_op jit(solution)/shard_map/ppermute | solution.py:117
  164.5 3.1 %collective-permute-done.33 = bf16[128,1024]{1,0:T(8,128)(2,1)S(1)} collective-permute-done((bf16[128,1024]{1,0:T(8,128)(2,1)S(1)}, bf16[128,1024]{1,0:T(8,128)(2,1)S(1)}, u32[]{:S(2)}, u32[]{:S(2)}) %collective-permute-start.33) | collective-permute-done | bytes 262176 | tf_op jit(solution)/shard_map/ppermute | solution.py:117
  167.6 6.0 %collective-permute-done.34 = bf16[128,1024]{1,0:T(8,128)(2,1)S(1)} collective-permute-done((bf16[128,1024]{1,0:T(8,128)(2,1)S(1)}, bf16[128,1024]{1,0:T(8,128)(2,1)S(1)}, u32[]{:S(2)}, u32[]{:S(2)}) %collective-permute-start.34) | collective-permute-done | bytes 262176 | tf_op jit(solution)/shard_map/ppermute | solution.py:117
  173.8 2.0 %copy-done.9 = bf16[128,16384]{1,0:T(8,128)(2,1)} copy-done((bf16[128,16384]{1,0:T(8,128)(2,1)}, bf16[128,16384]{1,0:T(8,128)(2,1)S(1)}, u32[]{:S(2)}) %copy-start.9) | copy-done | bytes 4194328
  (142 shorter events, 41.7 us)
Async XLA Ops:
  13.6 25.1 %collective-permute-start.10 = (bf16[2,128,768]{2,1,0:T(8,128)(2,1)S(1)}, bf16[2,128,768]{2,1,0:T(8,128)(2,1)S(1)}, u32[]{:S(2)}, u32[]{:S(2)}) collective-permute-start(bf16[2,128,768]{2,1,0:T(8,128)(2,1)S(1)} %get-tuple-element.62), channel_id=1, source_target_pairs={{0,2},{1,3},{2,0},{3,1},{4,6},{5,7},{6,4},{7,5},{8,10},{9,11},{10,... | collective-permute-start | bytes 1179656 | tf_op jit(solution)/shard_map/ppermute | solution.py:117
  15.1 24.0 %collective-permute-start.12 = (bf16[2,128,768]{2,1,0:T(8,128)(2,1)S(1)}, bf16[2,128,768]{2,1,0:T(8,128)(2,1)S(1)}, u32[]{:S(2)}, u32[]{:S(2)}) collective-permute-start(bf16[2,128,768]{2,1,0:T(8,128)(2,1)S(1)} %get-tuple-element.61), channel_id=1, source_target_pairs={{0,4},{1,5},{2,6},{3,7},{4,0},{5,1},{6,2},{7,3},{8,12},{9,13},{10,... | collective-permute-start | bytes 1179656 | tf_op jit(solution)/shard_map/ppermute | solution.py:117
  16.7 22.6 %collective-permute-start.14 = (bf16[2,128,768]{2,1,0:T(8,128)(2,1)S(1)}, bf16[2,128,768]{2,1,0:T(8,128)(2,1)S(1)}, u32[]{:S(2)}, u32[]{:S(2)}) collective-permute-start(bf16[2,128,768]{2,1,0:T(8,128)(2,1)S(1)} %get-tuple-element.60), channel_id=1, source_target_pairs={{0,6},{1,7},{2,4},{3,5},{4,2},{5,3},{6,0},{7,1},{8,14},{9,15},{10,... | collective-permute-start | bytes 1179656 | tf_op jit(solution)/shard_map/ppermute | solution.py:117
  17.1 20.8 %collective-permute-start.24 = (bf16[128,1024]{1,0:T(8,128)(2,1)S(1)}, bf16[128,1024]{1,0:T(8,128)(2,1)S(1)}, u32[]{:S(2)}, u32[]{:S(2)}) collective-permute-start(bf16[128,1024]{1,0:T(8,128)(2,1)S(1)} %get-tuple-element.48), channel_id=1, source_target_pairs={{0,2},{1,3},{2,0},{3,1},{4,6},{5,7},{6,4},{7,5},{8,10},{9,11},{10,... | collective-permute-start | bytes 786440 | tf_op jit(solution)/shard_map/ppermute | solution.py:117
  19.3 20.4 %collective-permute-start = (bf16[128,1024]{1,0:T(8,128)(2,1)}, bf16[128,1024]{1,0:T(8,128)(2,1)}, u32[]{:S(2)}, u32[]{:S(2)}) collective-permute-start(bf16[128,1024]{1,0:T(8,128)(2,1)} %get-tuple-element.57), channel_id=1, source_target_pairs={{0,1},{1,0},{2,3},{3,2},{4,5},{5,4},{6,7},{7,6},{8,9},{9,8},{10,11... | collective-permute-start | bytes 786440 | tf_op jit(solution)/shard_map/ppermute | solution.py:117
  49.2 19.3 %collective-permute-start.3 = (bf16[128,1024]{1,0:T(8,128)(2,1)}, bf16[128,1024]{1,0:T(8,128)(2,1)}, u32[]{:S(2)}, u32[]{:S(2)}) collective-permute-start(bf16[128,1024]{1,0:T(8,128)(2,1)} %get-tuple-element.54), channel_id=1, source_target_pairs={{0,4},{1,5},{2,6},{3,7},{4,0},{5,1},{6,2},{7,3},{8,12},{9,13},{10,... | collective-permute-start | bytes 786440 | tf_op jit(solution)/shard_map/ppermute | solution.py:117
  50.7 25.2 %collective-permute-start.4 = (bf16[128,1024]{1,0:T(8,128)(2,1)}, bf16[128,1024]{1,0:T(8,128)(2,1)}, u32[]{:S(2)}, u32[]{:S(2)}) collective-permute-start(bf16[128,1024]{1,0:T(8,128)(2,1)} %get-tuple-element.53), channel_id=1, source_target_pairs={{0,5},{1,4},{2,7},{3,6},{4,1},{5,0},{6,3},{7,2},{8,13},{9,12},{10,... | collective-permute-start | bytes 786440 | tf_op jit(solution)/shard_map/ppermute | solution.py:117
  51.9 24.6 %collective-permute-start.5 = (bf16[128,1024]{1,0:T(8,128)(2,1)}, bf16[128,1024]{1,0:T(8,128)(2,1)}, u32[]{:S(2)}, u32[]{:S(2)}) collective-permute-start(bf16[128,1024]{1,0:T(8,128)(2,1)} %get-tuple-element.52), channel_id=1, source_target_pairs={{0,6},{1,7},{2,4},{3,5},{4,2},{5,3},{6,0},{7,1},{8,14},{9,15},{10,... | collective-permute-start | bytes 786440 | tf_op jit(solution)/shard_map/ppermute | solution.py:117
  53.4 24.3 %collective-permute-start.6 = (bf16[128,1024]{1,0:T(8,128)(2,1)}, bf16[128,1024]{1,0:T(8,128)(2,1)}, u32[]{:S(2)}, u32[]{:S(2)}) collective-permute-start(bf16[128,1024]{1,0:T(8,128)(2,1)} %get-tuple-element.51), channel_id=1, source_target_pairs={{0,7},{1,6},{2,5},{3,4},{4,3},{5,2},{6,1},{7,0},{8,15},{9,14},{10,... | collective-permute-start | bytes 786440 | tf_op jit(solution)/shard_map/ppermute | solution.py:117
  61.3 30.5 %collective-permute-start.25 = (bf16[128,1024]{1,0:T(8,128)(2,1)S(1)}, bf16[128,1024]{1,0:T(8,128)(2,1)S(1)}, u32[]{:S(2)}, u32[]{:S(2)}) collective-permute-start(bf16[128,1024]{1,0:T(8,128)(2,1)S(1)} %copy-done.16), channel_id=1, source_target_pairs={{0,3},{1,2},{2,1},{3,0},{4,7},{5,6},{6,5},{7,4},{8,11},{9,10},{10,... | collective-permute-start | bytes 786440 | tf_op jit(solution)/shard_map/ppermute | solution.py:117
  68.5 23.3 %collective-permute-start.26 = (bf16[128,1024]{1,0:T(8,128)(2,1)S(1)}, bf16[128,1024]{1,0:T(8,128)(2,1)S(1)}, u32[]{:S(2)}, u32[]{:S(2)}) collective-permute-start(bf16[128,1024]{1,0:T(8,128)(2,1)S(1)} %copy-done.15), channel_id=1, source_target_pairs={{0,4},{1,5},{2,6},{3,7},{4,0},{5,1},{6,2},{7,3},{8,12},{9,13},{10,... | collective-permute-start | bytes 786440 | tf_op jit(solution)/shard_map/ppermute | solution.py:117
  75.9 22.0 %collective-permute-start.27 = (bf16[128,1024]{1,0:T(8,128)(2,1)S(1)}, bf16[128,1024]{1,0:T(8,128)(2,1)S(1)}, u32[]{:S(2)}, u32[]{:S(2)}) collective-permute-start(bf16[128,1024]{1,0:T(8,128)(2,1)S(1)} %copy-done.14), channel_id=1, source_target_pairs={{0,5},{1,4},{2,7},{3,6},{4,1},{5,0},{6,3},{7,2},{8,13},{9,12},{10,... | collective-permute-start | bytes 786440 | tf_op jit(solution)/shard_map/ppermute | solution.py:117
  76.4 21.5 %collective-permute-start.28 = (bf16[128,1024]{1,0:T(8,128)(2,1)S(1)}, bf16[128,1024]{1,0:T(8,128)(2,1)S(1)}, u32[]{:S(2)}, u32[]{:S(2)}) collective-permute-start(bf16[128,1024]{1,0:T(8,128)(2,1)S(1)} %copy-done.13), channel_id=1, source_target_pairs={{0,6},{1,7},{2,4},{3,5},{4,2},{5,3},{6,0},{7,1},{8,14},{9,15},{10,... | collective-permute-start | bytes 786440 | tf_op jit(solution)/shard_map/ppermute | solution.py:117
  77.6 20.3 %collective-permute-start.29 = (bf16[128,1024]{1,0:T(8,128)(2,1)S(1)}, bf16[128,1024]{1,0:T(8,128)(2,1)S(1)}, u32[]{:S(2)}, u32[]{:S(2)}) collective-permute-start(bf16[128,1024]{1,0:T(8,128)(2,1)S(1)} %copy-done.12), channel_id=1, source_target_pairs={{0,7},{1,6},{2,5},{3,4},{4,3},{5,2},{6,1},{7,0},{8,15},{9,14},{10,... | collective-permute-start | bytes 786440 | tf_op jit(solution)/shard_map/ppermute | solution.py:117
  109.5 46.1 %collective-permute-start.30 = (bf16[128,1024]{1,0:T(8,128)(2,1)S(1)}, bf16[128,1024]{1,0:T(8,128)(2,1)S(1)}, u32[]{:S(2)}, u32[]{:S(2)}) collective-permute-start(bf16[128,1024]{1,0:T(8,128)(2,1)S(1)} %get-tuple-element.34), channel_id=1, source_target_pairs={{0,2},{1,3},{2,0},{3,1},{4,6},{5,7},{6,4},{7,5},{8,10},{9,11},{10,... | collective-permute-start | bytes 786440 | tf_op jit(solution)/shard_map/ppermute | solution.py:117
  110.1 27.5 %collective-permute-start.16 = (bf16[128,1024]{1,0:T(8,128)(2,1)}, bf16[128,1024]{1,0:T(8,128)(2,1)}, u32[]{:S(2)}, u32[]{:S(2)}) collective-permute-start(bf16[128,1024]{1,0:T(8,128)(2,1)} %get-tuple-element.26), channel_id=1, source_target_pairs={{0,2},{1,3},{2,0},{3,1},{4,6},{5,7},{6,4},{7,5},{8,10},{9,11},{10,... | collective-permute-start | bytes 786440 | tf_op jit(solution)/shard_map/ppermute | solution.py:117
  111.5 29.5 %collective-permute-start.17 = (bf16[128,1024]{1,0:T(8,128)(2,1)}, bf16[128,1024]{1,0:T(8,128)(2,1)}, u32[]{:S(2)}, u32[]{:S(2)}) collective-permute-start(bf16[128,1024]{1,0:T(8,128)(2,1)} %get-tuple-element.27), channel_id=1, source_target_pairs={{0,4},{1,5},{2,6},{3,7},{4,0},{5,1},{6,2},{7,3},{8,12},{9,13},{10,... | collective-permute-start | bytes 786440 | tf_op jit(solution)/shard_map/ppermute | solution.py:117
  113.0 29.7 %collective-permute-start.18 = (bf16[128,1024]{1,0:T(8,128)(2,1)}, bf16[128,1024]{1,0:T(8,128)(2,1)}, u32[]{:S(2)}, u32[]{:S(2)}) collective-permute-start(bf16[128,1024]{1,0:T(8,128)(2,1)} %get-tuple-element.28), channel_id=1, source_target_pairs={{0,6},{1,7},{2,4},{3,5},{4,2},{5,3},{6,0},{7,1},{8,14},{9,15},{10,... | collective-permute-start | bytes 786440 | tf_op jit(solution)/shard_map/ppermute | solution.py:117
  113.6 16.1 %collective-permute-start.38 = (f32[32,128]{1,0:T(8,128)S(1)}, f32[32,128]{1,0:T(8,128)S(1)}, u32[]{:S(2)}, u32[]{:S(2)}) collective-permute-start(f32[32,128]{1,0:T(8,128)S(1)} %pad_maximum_fusion.4), channel_id=1, source_target_pairs={{0,2},{1,3},{2,0},{3,1},{4,6},{5,7},{6,4},{7,5},{8,10},{9,11},{10,... | collective-permute-start | bytes 49160 | tf_op jit(solution)/shard_map/ppermute | solution.py:117
  137.6 14.4 %collective-permute-start.20 = (bf16[128,1024]{1,0:T(8,128)(2,1)S(1)}, bf16[128,1024]{1,0:T(8,128)(2,1)S(1)}, u32[]{:S(2)}, u32[]{:S(2)}) collective-permute-start(bf16[128,1024]{1,0:T(8,128)(2,1)S(1)} %get-tuple-element.30), channel_id=1, source_target_pairs={{0,5},{1,4},{2,7},{3,6},{4,1},{5,0},{6,3},{7,2},{8,13},{9,12},{10,... | collective-permute-start | bytes 786440 | tf_op jit(solution)/shard_map/ppermute | solution.py:117
  144.4 20.0 %collective-permute-start.31 = (bf16[128,1024]{1,0:T(8,128)(2,1)S(1)}, bf16[128,1024]{1,0:T(8,128)(2,1)S(1)}, u32[]{:S(2)}, u32[]{:S(2)}) collective-permute-start(bf16[128,1024]{1,0:T(8,128)(2,1)S(1)} %get-tuple-element.35), channel_id=1, source_target_pairs={{0,4},{1,5},{2,6},{3,7},{4,0},{5,1},{6,2},{7,3},{8,12},{9,13},{10,... | collective-permute-start | bytes 786440 | tf_op jit(solution)/shard_map/ppermute | solution.py:117
  153.2 14.4 %collective-permute-start.33 = (bf16[128,1024]{1,0:T(8,128)(2,1)S(1)}, bf16[128,1024]{1,0:T(8,128)(2,1)S(1)}, u32[]{:S(2)}, u32[]{:S(2)}) collective-permute-start(bf16[128,1024]{1,0:T(8,128)(2,1)S(1)} %get-tuple-element.37), channel_id=1, source_target_pairs={{0,3},{1,2},{2,1},{3,0},{4,7},{5,6},{6,5},{7,4},{8,11},{9,10},{10,... | collective-permute-start | bytes 786440 | tf_op jit(solution)/shard_map/ppermute | solution.py:117
  155.3 18.4 %collective-permute-start.34 = (bf16[128,1024]{1,0:T(8,128)(2,1)S(1)}, bf16[128,1024]{1,0:T(8,128)(2,1)S(1)}, u32[]{:S(2)}, u32[]{:S(2)}) collective-permute-start(bf16[128,1024]{1,0:T(8,128)(2,1)S(1)} %get-tuple-element.38), channel_id=1, source_target_pairs={{0,5},{1,4},{2,7},{3,6},{4,1},{5,0},{6,3},{7,2},{8,13},{9,12},{10,... | collective-permute-start | bytes 786440 | tf_op jit(solution)/shard_map/ppermute | solution.py:117
  155.5 18.2 %collective-permute-start.35 = (bf16[128,1024]{1,0:T(8,128)(2,1)S(1)}, bf16[128,1024]{1,0:T(8,128)(2,1)S(1)}, u32[]{:S(2)}, u32[]{:S(2)}) collective-permute-start(bf16[128,1024]{1,0:T(8,128)(2,1)S(1)} %get-tuple-element.39), channel_id=1, source_target_pairs={{0,7},{1,6},{2,5},{3,4},{4,3},{5,2},{6,1},{7,0},{8,15},{9,14},{10,... | collective-permute-start | bytes 786440 | tf_op jit(solution)/shard_map/ppermute | solution.py:117
  (36 other events, 393.7 us)
where the time goes:
time: 177 us; the launch traced here: 176 us
  waiting for transfers between devices  82.2 us (46%)
  starting transfers between devices  43.9 us (25%)
  Pallas kernels  27.8 us (16%)
  local copies, waits for them, and re-layouts  18.5 us (10%)
  other arithmetic  2.31 us (1%)
    ppermute x38, waiting for transfers between devices, partner(): return lax.ppermute(x, 'mem', [(i, i ^ flip) for i in range(count)])  80.9 us
    ppermute x38, starting transfers between devices, partner(): return lax.ppermute(x, 'mem', [(i, i ^ flip) for i in range(count)])  37.7 us
    pallas_call x2, Pallas kernels, analyse(): pl.pallas_call(functools.partial(analyse_kernel, count, rows, span, obs_l...  23.4 us
    unnamed x45, local copies, waits for them, and re-layouts  8.98 us
    ppermute x1, starting transfers between devices, per_device(): before = lax.ppermute(both[:, :, -rim:], 'band', up)  4.94 us
    dynamic_update_slice x16, local copies, waits for them, and re-layouts, per_device(): analysis = lax.dynamic_update_slice(analysis, piece, (0, first))  4.15 us
    dynamic_slice x1, local copies, waits for them, and re-layouts, outgoing(): return lax.dynamic_slice_in_dim(prior_ensemble, first, chunk_span, 1)  4.03 us
  transfers between devices with their start and end apart: 40, of which 12 were waited for; matrix products, arithmetic and copies ran while one was open for 7% of the time, Pallas kernels for 9%

commit v1 on v0

v1 whole, which is shorter than its diff:
```python
import functools

import jax
import jax.numpy as jnp
from jax import lax
from jax.experimental import pallas as pl
from jax.experimental.pallas import tpu as pltpu
from jax.sharding import PartitionSpec as P

RIM_BLOCKS = 2
CHUNKS = 2
STEP_PATCHES = 4
PAD_ROWS = 16
VMEM_BYTES = 60 * 1024 * 1024
IN_FLIGHT = 4
FIRST = 3
EARLY = 3
ASSEMBLE_BEFORE = 4


def taper_kernel(scale, loc_ref, taper_ref):
    for i in range(loc_ref.shape[0]):
        taper_ref[i] = jnp.transpose(loc_ref[i]) * scale


def assemble_kernel(moves, span, place_ref, *refs):
    pieces, (out_ref, sems) = refs[: len(moves)], refs[-2:]
    copies = []
    for i, (flip, stride, first) in enumerate(moves):
        column = jnp.bitwise_xor(place_ref[0], flip) * stride + first
        there = out_ref.at[:, pl.ds(pl.multiple_of(column, span), pieces[i].shape[1])]
        copies.append(pltpu.make_async_copy(pieces[i], there, sems.at[i]))
        copies[-1].start()
    for copy in copies:
        copy.wait()


def prepare_kernel(count, rows, width, centres, obs_len, place_ref, *refs):
    pieces, (ydt_ref, solved_ref, ysum_ref) = refs[:count], refs[count:]
    offset = pl.multiple_of((place_ref[0] & 1) * (centres * obs_len), obs_len)
    window = pl.ds(offset, width)
    members = count * rows
    total = jnp.zeros((1, width), jnp.float32)
    for piece in pieces:
        total = total + jnp.sum(piece[0, :, window].astype(jnp.float32), axis=0, keepdims=True)
    centre = total / members
    for i, piece in enumerate(pieces):
        place = slice(i * rows, (i + 1) * rows)
        dev = piece[0, :, window].astype(jnp.float32) - centre
        ydt_ref[:width, place] = jnp.transpose(dev).astype(jnp.bfloat16)
        solved_ref[place, :] = piece[1, :, window]
    ydt_ref[width:, :] = jnp.ones((ydt_ref.shape[0] - width, members), jnp.bfloat16)
    ysum_ref[...] = jnp.dot(
        ydt_ref[:width, :],
        jnp.ones((members, ysum_ref.shape[1]), jnp.bfloat16),
        preferred_element_type=jnp.float32,
    )


def analyse_kernel(count, rows, span, obs_len, start, geometry, place_ref, block_ref, taper_ref, *refs):
    priors, (ydt_ref, solved_ref, ysum_ref, loc_ref) = refs[:count], refs[count : count + 4]
    outs, (var_ref, weight_ref) = refs[count + 4 : 2 * count + 4], refs[2 * count + 4 :]
    step = pl.program_id(0)
    per_worker, centres, band_blocks = geometry
    first_patch = place_ref[0] * per_worker + start
    first_block = place_ref[1] * band_blocks + place_ref[0] * centres - RIM_BLOCKS
    width = solved_ref.shape[1]
    members = count * rows
    patches = priors[0].shape[1] // span
    weight_ref[...] = jnp.zeros_like(weight_ref)
    for j in range(patches):
        patch = first_patch + step * patches + j
        for k in range(block_ref.shape[0]):
            row = pl.multiple_of((block_ref[k, patch] - first_block) * obs_len, obs_len)
            there = (pl.ds(row, obs_len), slice(j * span, (j + 1) * span))
            weight_ref[there] = weight_ref[there] + loc_ref[taper_ref[k, patch]]
    prior = jnp.concatenate([ref[...] for ref in priors], axis=0)
    product = jnp.dot(ydt_ref[...], prior, preferred_element_type=jnp.float32)
    mean = product[width : width + 1, :] * (1.0 / members)
    ysum = jnp.concatenate([ysum_ref[...]] * patches, axis=1)
    cov = product[:width, :] - ysum * mean
    tapered = (cov * weight_ref[...]).astype(jnp.bfloat16)
    increment = jnp.dot(solved_ref[...], tapered, preferred_element_type=jnp.float32)
    updated = (prior.astype(jnp.float32) + increment).astype(jnp.bfloat16)
    for i, out in enumerate(outs):
        out[...] = updated[i * rows : (i + 1) * rows, :]
    updated = updated.astype(jnp.float32)
    centre = jnp.sum(updated, axis=0, keepdims=True) * (1.0 / members)
    variance = jnp.sum((updated - centre) ** 2, axis=0, keepdims=True) * (1.0 / members)
    for j in range(patches):
        var_ref[pl.ds(step * patches + j, 1), :] = variance[:, j * span : (j + 1) * span]


def select_kernel(per_worker, owner_ref, place_ref, out_ref):
    me = place_ref[0]
    out_ref[...] = jnp.zeros_like(out_ref)
    lanes = lax.broadcasted_iota(jnp.int32, (1, out_ref.shape[1]), 1)

    def one(patch, filled):
        mine = owner_ref[patch] == me

        @pl.when(mine)
        def _():
            source = jnp.bitwise_xor(patch // per_worker, me) * per_worker + patch % per_worker
            out_ref[pl.ds(filled, 1), :] = (lanes == source).astype(jnp.float32)

        return filled + mine.astype(jnp.int32)

    lax.fori_loop(0, owner_ref.shape[0], one, jnp.int32(0))


def spread_kernel(select_ref, var_ref, out_ref):
    out_ref[...] = jnp.dot(
        select_ref[...],
        var_ref[...],
        precision=lax.Precision.HIGHEST,
        preferred_element_type=jnp.float32,
    )


def whole(shape):
    return pl.BlockSpec(shape, lambda *_: (0,) * len(shape))


def per_device(
    prior_ensemble,
    perturbed_measurements,
    solved_residuals,
    localisation_matrix,
    piece_owner_device,
    measurement_group_matrix,
    localisation_factors,
):
    rows, vector_span = prior_ensemble.shape
    taper_count, span, obs_len = localisation_matrix.shape
    count, bands = lax.axis_size("mem"), lax.axis_size("band")
    members = rows * count
    strip = vector_span // span
    band_blocks = perturbed_measurements.shape[1] // obs_len
    per_worker = strip // count
    centres = per_worker * band_blocks // strip
    assert centres * strip == per_worker * band_blocks and count & (count - 1) == 0
    window = 2 * RIM_BLOCKS + centres
    width = window * obs_len
    strip_position = lax.axis_index("band")
    me = lax.axis_index("mem")

    place = jnp.stack([me, strip_position]).astype(jnp.int32)
    sent = []

    def after_sent(x):
        if len(sent) >= IN_FLIGHT:
            x, sent[-IN_FLIGHT] = lax.optimization_barrier((x, sent[-IN_FLIGHT]))
        return x

    def partner(x, flip):
        pairs = [(i, i ^ flip) for i in range(count)]
        if flip == 1:
            return lax.ppermute(x, "mem", pairs)
        sent.append(lax.ppermute(after_sent(x), "mem", pairs))
        return sent[-1]

    pair_width = (window + centres) * obs_len

    chunk_patches = per_worker // CHUNKS
    chunk_span = chunk_patches * span

    select = pl.pallas_call(
        functools.partial(select_kernel, per_worker),
        grid_spec=pltpu.PrefetchScalarGridSpec(
            num_scalar_prefetch=2,
            grid=(1,),
            in_specs=[],
            out_specs=whole((2 * per_worker, strip)),
        ),
        out_shape=jax.ShapeDtypeStruct((2 * per_worker, strip), jnp.float32),
    )(piece_owner_device, place)
    taper = pl.pallas_call(
        functools.partial(taper_kernel, 1.0 / (members - 1)),
        out_shape=jax.ShapeDtypeStruct((taper_count, obs_len, span), jnp.float32),
        compiler_params=pltpu.CompilerParams(vmem_limit_bytes=VMEM_BYTES),
    )(localisation_matrix)

    order = list(range(2, count, 2)) + list(range(3, count, 2)) + [1]

    def outgoing(source, flip, chunk):
        first = (me ^ flip) * (per_worker * span) + chunk * chunk_span
        return lax.dynamic_slice_in_dim(source, first, chunk_span, 1)

    source, cut = prior_ensemble, []
    got = [{} for _ in range(CHUNKS)]
    for flip in order[:FIRST]:
        cut.append(outgoing(source, flip, 0))
        source, cut[-1] = lax.optimization_barrier((source, cut[-1]))
        got[0][flip] = partner(cut[-1], flip)
    both = jnp.stack([perturbed_measurements, solved_residuals])
    both, got[0][order[0]] = lax.optimization_barrier((both, got[0][order[0]]))
    up = [(i, i + 1) for i in range(bands - 1)]
    down = [(j, i) for i, j in up]
    rim = RIM_BLOCKS * obs_len
    before = lax.ppermute(both[:, :, -rim:], "band", up)
    after = lax.ppermute(both[:, :, :rim], "band", down)
    padded = jnp.concatenate([before, both, after], axis=2)

    def pair_window(flip):
        first = ((me ^ flip) >> 1) * (2 * centres * obs_len)
        return lax.dynamic_slice_in_dim(padded, first, pair_width, 2)

    for flip in order[FIRST:]:
        got[0][flip] = partner(outgoing(source, flip, 0), flip)
    even = {0: pair_window(0)}
    for flip in range(2, count, 2):
        even[flip] = partner(pair_window(flip), flip)
    for flip in order[:EARLY]:
        got[1][flip] = partner(outgoing(source, flip, 1), flip)
    even[0], select, taper = lax.optimization_barrier((even[0], select, taper))
    pieces = []
    for flip in range(0, count, 2):
        pieces += [even[flip], partner(even[flip], 1)]
    for chunk in range(1, CHUNKS):
        for flip in order:
            if flip not in got[chunk]:
                got[chunk][flip] = partner(outgoing(source, flip, chunk), flip)
    priors = [[pieces_of[i] for i in range(1, count)] for pieces_of in got]

    ydt, solved, ysum = pl.pallas_call(
        functools.partial(prepare_kernel, count, rows, width, centres, obs_len),
        grid_spec=pltpu.PrefetchScalarGridSpec(
            num_scalar_prefetch=1,
            grid=(1,),
            in_specs=[whole((2, rows, pair_width))] * count,
            out_specs=[
                whole((width + PAD_ROWS, members)),
                whole((members, width)),
                whole((width, span)),
            ],
        ),
        out_shape=[
            jax.ShapeDtypeStruct((width + PAD_ROWS, members), jnp.bfloat16),
            jax.ShapeDtypeStruct((members, width), jnp.bfloat16),
            jax.ShapeDtypeStruct((width, span), jnp.float32),
        ],
        compiler_params=pltpu.CompilerParams(vmem_limit_bytes=VMEM_BYTES),
        cost_estimate=pl.CostEstimate(
            flops=20 * members * width, bytes_accessed=8 * members * width, transcendentals=0
        ),
    )(place, *pieces)

    step_span = STEP_PATCHES * span
    piece_spec = pl.BlockSpec((rows, step_span), lambda i, *_: (0, i))
    blocks, tapers = measurement_group_matrix.T, localisation_factors.T

    def analyse(chunk, prior):
        steps = chunk_patches // STEP_PATCHES

        def own(i, place_ref, *_):
            return 0, (place_ref[0] * CHUNKS + chunk) * steps + i

        *out, variance = pl.pallas_call(
            functools.partial(
                analyse_kernel,
                count,
                rows,
                span,
                obs_len,
                chunk * chunk_patches,
                (per_worker, centres, band_blocks),
            ),
            grid_spec=pltpu.PrefetchScalarGridSpec(
                num_scalar_prefetch=3,
                grid=(steps,),
                in_specs=[pl.BlockSpec((rows, step_span), own)]
                + [piece_spec] * (count - 1)
                + [
                    whole((width + PAD_ROWS, members)),
                    whole((members, width)),
                    whole((width, span)),
                    whole((taper_count, obs_len, span)),
                ],
                out_specs=[piece_spec] * count + [whole((chunk_patches, span))],
                scratch_shapes=[pltpu.VMEM((width, step_span), jnp.float32)],
            ),
            out_shape=[jax.ShapeDtypeStruct((rows, chunk_span), jnp.bfloat16)] * count
            + [jax.ShapeDtypeStruct((chunk_patches, span), jnp.float32)],
            compiler_params=pltpu.CompilerParams(vmem_limit_bytes=VMEM_BYTES),
            cost_estimate=pl.CostEstimate(
                flops=4 * members * width * chunk_span,
                bytes_accessed=4 * members * (width + chunk_span),
                transcendentals=0,
            ),
        )(place, blocks, tapers, prior_ensemble, *prior, ydt, solved, ysum, taper)
        return out, variance

    def assemble(analysis, pieces, moves):
        base = [] if analysis is None else [analysis]
        return pl.pallas_call(
            functools.partial(assemble_kernel, moves, span),
            grid_spec=pltpu.PrefetchScalarGridSpec(
                num_scalar_prefetch=1,
                grid=(1,),
                in_specs=[whole((rows, chunk_span))] * len(pieces)
                + [pl.BlockSpec(memory_space=pl.ANY)] * len(base),
                out_specs=pl.BlockSpec(memory_space=pl.ANY),
                scratch_shapes=[pltpu.SemaphoreType.DMA((len(pieces),))],
            ),
            out_shape=jax.ShapeDtypeStruct(prior_ensemble.shape, prior_ensemble.dtype),
            input_output_aliases={1 + len(pieces): 0} if base else {},
            compiler_params=pltpu.CompilerParams(vmem_limit_bytes=VMEM_BYTES),
            cost_estimate=pl.CostEstimate(
                flops=0, bytes_accessed=4 * len(pieces) * rows * chunk_span, transcendentals=0
            ),
        )(place, *pieces, *base)

    analysis = None
    gathered, spread_flip = [], 1
    back = order
    for chunk in range(CHUNKS):
        out, variance = analyse(chunk, priors[chunk])
        gathered.append(variance)
        final = chunk == CHUNKS - 1
        arrived, moves = [], []
        for i, flip in enumerate([0] + back):
            if final and spread_flip < count:
                if spread_flip == 1:
                    gathered = jnp.concatenate(gathered, axis=0)
                gathered = jnp.concatenate([gathered, partner(gathered, spread_flip)], axis=0)
                spread_flip *= 2
            if final and i == ASSEMBLE_BEFORE:
                out[flip], analysis = lax.optimization_barrier((out[flip], analysis))
            arrived.append(partner(out[flip], flip) if flip else out[0])
            moves.append((flip, per_worker * span, chunk * chunk_span))
            if len(moves) == count or (final and len(moves) == count // 2 + 1):
                analysis = assemble(analysis, arrived, tuple(moves))
                arrived, moves = [], []
        if moves:
            analysis = assemble(analysis, arrived, tuple(moves))
    assert spread_flip == count
    spread = pl.pallas_call(
        spread_kernel,
        out_shape=jax.ShapeDtypeStruct((2 * per_worker, span), jnp.float32),
    )(select, gathered)
    return analysis, spread


def solution(mesh):
    return jax.shard_map(
        per_device,
        mesh=mesh,
        in_specs=(
            P("mem", "band"),
            P("mem", "band"),
            P("mem", "band"),
            P(),
            P("band"),
            P("band", None),
            P("band", None),
        ),
        out_specs=(P("mem", "band"), P(("band", "mem"), None)),
        check_vma=False,
    )
```

time: 177 us -> 143 us (0.81)
  waiting for transfers between devices: 82.2 us -> 41.4 us
  Pallas kernels: 27.8 us -> 39.6 us
  local copies, waits for them, and re-layouts: 18.5 us -> 11.8 us
    ppermute x38, waiting for transfers between devices: 80.9 us -> 39.8 us  [the longest x29 39.1 us: partner(): sent.append(lax.ppermute(after_sent(x), 'mem', pairs))]
    pallas_call x2 -> x7, Pallas kernels: 4.34 us -> 21.1 us  [the longest x3 9.24 us: assemble(): pl.pallas_call(functools.partial(assemble_kernel, moves, span), grid_spec...]
    pallas_call x2, Pallas kernels: 23.4 us -> 18.4 us  [analyse(): pl.pallas_call(functools.partial(analyse_kernel, count, rows, span, obs_l...]
    unnamed x45 -> x74, local copies, waits for them, and re-layouts: 8.98 us -> 4.29 us
    dynamic_update_slice x16 -> x0, local copies, waits for them, and re-layouts: 4.15 us -> none  [per_device(): analysis = lax.dynamic_update_slice(analysis, piece, (0, first))]
    dynamic_slice x1 -> x4, local copies, waits for them, and re-layouts: 4.03 us -> 7.36 us  [outgoing(): return lax.dynamic_slice_in_dim(source, first, chunk_span, 1)]
    concatenate x4 -> x3, other arithmetic: 0.06 us -> 2.14 us  [the longest x2 1.38 us: per_device(): jnp.concatenate([gathered, partner(gathered, spread_flip)], axis=0)]
    ppermute x38, starting transfers between devices: 37.7 us -> 39.7 us  [the longest x29 36.4 us: partner(): sent.append(lax.ppermute(after_sent(x), 'mem', pairs))]
  transfers between devices with their start and end apart: 40 -> 40, of which waited for: 12 -> 11; matrix products, arithmetic and copies ran while one was open for 7% -> 8% of each run, Pallas kernels for 9% -> 26%
where the time goes in v1:
time: 143 us; the launch traced here: 142 us
  starting transfers between devices  44.6 us (31%)
  waiting for transfers between devices  41.4 us (29%)
  Pallas kernels  39.6 us (28%)
  local copies, waits for them, and re-layouts  11.8 us (8%)
  other arithmetic  3.82 us (3%)
    ppermute x29, waiting for transfers between devices, partner(): sent.append(lax.ppermute(after_sent(x), 'mem', pairs))  39.1 us
    ppermute x29, starting transfers between devices, partner(): sent.append(lax.ppermute(after_sent(x), 'mem', pairs))  36.4 us
    pallas_call x2, Pallas kernels, analyse(): pl.pallas_call(functools.partial(analyse_kernel, count, rows, span, obs_l...  18.4 us
    pallas_call x3, Pallas kernels, assemble(): pl.pallas_call(functools.partial(assemble_kernel, moves, span), grid_spec...  9.24 us
    dynamic_slice x4, local copies, waits for them, and re-layouts, outgoing(): return lax.dynamic_slice_in_dim(source, first, chunk_span, 1)  7.36 us
    pallas_call x1, Pallas kernels, per_device(): pl.pallas_call(functools.partial(prepare_kernel, count, rows, width, cent...  4.98 us
    unnamed x74, local copies, waits for them, and re-layouts  4.29 us
    ppermute x1, starting transfers between devices, per_device(): before = lax.ppermute(both[:, :, -rim:], 'band', up)  3.67 us
  transfers between devices with their start and end apart: 40, of which 11 were waited for; matrix products, arithmetic and copies ran while one was open for 8% of the time, Pallas kernels for 26%

profile of v1, /device:TPU:0, one launch (start us, length us, event | category | flops | bytes accessed | tf_op | source)
XLA Modules:
  0.0 142.2 jit_solution(12079410828619708860)
XLA Ops:
  1.6 3.0 %collective-permute-start.4 = (bf16[128,1024]{1,0:T(8,128)(2,1)S(1)}, bf16[128,1024]{1,0:T(8,128)(2,1)S(1)}, u32[]{:S(2)}, u32[]{:S(2)}) collective-permute-start(bf16[128,1024]{1,0:T(8,128)(2,1)S(1)} %constant_dynamic-slice_fusion.17), channel_id=1, source_target_pairs={{0,2},{1,3},{2,0},{3,1},{4,6},{5,7},{6,4},{7,5},{8,10},{9,11},{10,... | collective-permute-start | bytes 786440 | tf_op jit(solution)/shard_map/ppermute | solution.py:160
  11.7 3.7 %collective-permute-start.5 = (bf16[2,128,256]{2,1,0:T(8,128)(2,1)S(1)}, bf16[2,128,256]{2,1,0:T(8,128)(2,1)S(1)}, u32[]{:S(2)}, u32[]{:S(2)}) collective-permute-start(bf16[2,128,256]{2,1,0:T(8,128)(2,1)S(1)} %get-tuple-element.136), channel_id=1, source_target_pairs={{0,8},{8,16},{16,24},{1,9},{9,17},{17,25},{2,10},{10,18},{18,26},{... | collective-permute-start | bytes 393224 | tf_op jit(solution)/shard_map/ppermute | solution.py:201
  15.4 3.1 %constant_dynamic-slice_fusion = (bf16[128,1024]{1,0:T(8,128)(2,1)}, bf16[128,1024]{1,0:T(8,128)(2,1)S(1)}, bf16[128,1024]{1,0:T(8,128)(2,1)}, bf16[128,1024]{1,...) fusion(bf16[128,16384]{1,0:T(8,128)(2,1)} %refs_0_.3, ...), kind=kLoop, calls=%fused_computation.12 | loop fusion | bytes 5767212 | tf_op jit(solution)/shard_map/dynamic_slice | solution.py:188
  19.7 3.9 %collective-permute-start.7 = (bf16[128,1024]{1,0:T(8,128)(2,1)S(1)}, bf16[128,1024]{1,0:T(8,128)(2,1)S(1)}, u32[]{:S(2)}, u32[]{:S(2)}) collective-permute-start(bf16[128,1024]{1,0:T(8,128)(2,1)S(1)} %get-tuple-element.69), channel_id=1, source_target_pairs={{0,5},{1,4},{2,7},{3,6},{4,1},{5,0},{6,3},{7,2},{8,13},{9,12},{10,... | collective-permute-start | bytes 786440 | tf_op jit(solution)/shard_map/ppermute | solution.py:160
  25.5 2.6 %collective-permute-start.11 = (bf16[2,128,768]{2,1,0:T(8,128)(2,1)S(1)}, bf16[2,128,768]{2,1,0:T(8,128)(2,1)S(1)}, u32[]{:S(2)}, u32[]{:S(2)}) collective-permute-start(bf16[2,128,768]{2,1,0:T(8,128)(2,1)S(1)} %get-tuple-element.73), channel_id=1, source_target_pairs={{0,2},{1,3},{2,0},{3,1},{4,6},{5,7},{6,4},{7,5},{8,10},{9,11},{10,... | collective-permute-start | bytes 1179656 | tf_op jit(solution)/shard_map/ppermute | solution.py:160
  28.1 2.4 %collective-permute-start.15 = (bf16[2,128,768]{2,1,0:T(8,128)(2,1)S(1)}, bf16[2,128,768]{2,1,0:T(8,128)(2,1)S(1)}, u32[]{:S(2)}, u32[]{:S(2)}) collective-permute-start(bf16[2,128,768]{2,1,0:T(8,128)(2,1)S(1)} %get-tuple-element.76), channel_id=1, source_target_pairs={{0,4},{1,5},{2,6},{3,7},{4,0},{5,1},{6,2},{7,3},{8,12},{9,13},{10,... | collective-permute-start | bytes 1179656 | tf_op jit(solution)/shard_map/ppermute | solution.py:160
  32.9 2.1 %shard_map.87.refs_11_ = f32[8,128,128]{2,1,0:T(8,128)} custom-call(f32[8,128,128]{2,1,0:T(8,128)} %loc_ref.1), custom_call_target="tpu_custom_call" | custom-call | tf_op jit(solution)/shard_map/pallas_call | solution.py:178
  35.6 3.2 %shard_map.86.select_ref = f32[32,128]{1,0:T(8,128)} custom-call(s32[128]{0:T(128)} %owner_ref.1, s32[2]{0:T(128)} %pad_add_fusion.place_ref), custom_call_target="tpu_custom_call" | custom-call | tf_op jit(solution)/shard_map/pallas_call | solution.py:168
  39.4 14.6 %collective-permute-done.2.refs_7_ = bf16[128,1024]{1,0:T(8,128)(2,1)} collective-permute-done((bf16[128,1024]{1,0:T(8,128)(2,1)}, bf16[128,1024]{1,0:T(8,128)(2,1)}, u32[]{:S(2)}, u32[]{:S(2)}) %collective-permute-start.2) | collective-permute-done | bytes 262176 | tf_op jit(solution)/shard_map/ppermute | solution.py:160
  55.4 7.0 %collective-permute-done.3.refs_2_ = bf16[128,1024]{1,0:T(8,128)(2,1)S(1)} collective-permute-done((bf16[128,1024]{1,0:T(8,128)(2,1)}, bf16[128,1024]{1,0:T(8,128)(2,1)S(1)}, u32[]{:S(2)}, u32[]{:S(2)}) %collective-permute-start.3) | collective-permute-done | bytes 262176 | tf_op jit(solution)/shard_map/ppermute | solution.py:160
  68.1 5.0 %shard_map.88 = (bf16[656,1024]{1,0:T(8,128)(2,1)}, bf16[1024,640]{1,0:T(8,128)(2,1)}, f32[640,128]{1,0:T(8,128)}) custom-call(s32[2]{0:T(128)} %pad_add_fusion.place_ref, bf16[2,128,768]{2,1,0:T(8,128)(2,1)} %copy-done, bf16[2,128,768]{2,1,0:T(8,128)(2,1)} %copy-done.4, bf16[2,128,768]{2,1,0:T(8,128)(2,1)} %copy-done.1, bf16[2,128,768]{2,1,0:T(8,128)(2,1)} %copy-done.5, ...), custom_call_target="tpu_custom_call" | custom-call | flops 13107200 | bytes 5242880 | tf_op jit(solution)/shard_map/pallas_call | solution.py:226
  73.1 9.2 %shard_map.90 = (bf16[128,1024]{1,0:T(8,128)(2,1)}, bf16[128,1024]{1,0:T(8,128)(2,1)}, bf16[128,1024]{1,0:T(8,128)(2,1)}, bf16[128,1024]{1,0:T(8,128)(2,1)}, bf1...) custom-call(s32[2]{0:T(128)} %pad_add_fusion.place_ref, ...), custom_call_target="tpu_custom_call" | custom-call | flops 2684354560 | bytes 6815744 | tf_op jit(solution)/shard_map/pallas_call | solution.py:259
  88.0 3.5 %collective-permute-done.30.refs_2_ = bf16[128,1024]{1,0:T(8,128)(2,1)S(1)} collective-permute-done((bf16[128,1024]{1,0:T(8,128)(2,1)}, bf16[128,1024]{1,0:T(8,128)(2,1)S(1)}, u32[]{:S(2)}, u32[]{:S(2)}) %collective-permute-start.30) | collective-permute-done | bytes 262176 | tf_op jit(solution)/shard_map/ppermute | solution.py:160
  92.6 9.2 %shard_map.89 = (bf16[128,1024]{1,0:T(8,128)(2,1)}, bf16[128,1024]{1,0:T(8,128)(2,1)}, bf16[128,1024]{1,0:T(8,128)(2,1)}, bf16[128,1024]{1,0:T(8,128)(2,1)}, bf1...) custom-call(s32[2]{0:T(128)} %pad_add_fusion.place_ref, ...), custom_call_target="tpu_custom_call" | custom-call | flops 2684354560 | bytes 6815744 | tf_op jit(solution)/shard_map/pallas_call | solution.py:259
  105.6 1.7 %collective-permute-start.36 = (bf16[128,1024]{1,0:T(8,128)(2,1)}, bf16[128,1024]{1,0:T(8,128)(2,1)S(1)}, u32[]{:S(2)}, u32[]{:S(2)}) collective-permute-start(bf16[128,1024]{1,0:T(8,128)(2,1)} %get-tuple-element.110), channel_id=1, source_target_pairs={{0,2},{1,3},{2,0},{3,1},{4,6},{5,7},{6,4},{7,5},{8,10},{9,11},{10,... | collective-permute-start | bytes 786440 | tf_op jit(solution)/shard_map/ppermute | solution.py:160
  107.7 1.7 %collective-permute-done.31.refs_6_ = bf16[128,1024]{1,0:T(8,128)(2,1)S(1)} collective-permute-done((bf16[128,1024]{1,0:T(8,128)(2,1)}, bf16[128,1024]{1,0:T(8,128)(2,1)S(1)}, u32[]{:S(2)}, u32[]{:S(2)}) %collective-permute-start.31) | collective-permute-done | bytes 262176 | tf_op jit(solution)/shard_map/ppermute | solution.py:160
  109.4 2.1 %collective-permute-start.32 = (bf16[128,1024]{1,0:T(8,128)(2,1)}, bf16[128,1024]{1,0:T(8,128)(2,1)S(1)}, u32[]{:S(2)}, u32[]{:S(2)}) collective-permute-start(bf16[128,1024]{1,0:T(8,128)(2,1)} %get-tuple-element.103), channel_id=1, source_target_pairs={{0,4},{1,5},{2,6},{3,7},{4,0},{5,1},{6,2},{7,3},{8,12},{9,13},{10,... | collective-permute-start | bytes 786440 | tf_op jit(solution)/shard_map/ppermute | solution.py:160
  111.5 4.7 %collective-permute-done.25 = f32[32,128]{1,0:T(8,128)S(1)} collective-permute-done((f32[32,128]{1,0:T(8,128)S(1)}, f32[32,128]{1,0:T(8,128)S(1)}, u32[]{:S(2)}, u32[]{:S(2)}) %collective-permute-start.25) | collective-permute-done | bytes 16416 | tf_op jit(solution)/shard_map/ppermute | solution.py:160
  118.0 2.1 %collective-permute-start.37 = (bf16[128,1024]{1,0:T(8,128)(2,1)}, bf16[128,1024]{1,0:T(8,128)(2,1)S(1)}, u32[]{:S(2)}, u32[]{:S(2)}) collective-permute-start(bf16[128,1024]{1,0:T(8,128)(2,1)} %get-tuple-element.112), channel_id=1, source_target_pairs={{0,6},{1,7},{2,4},{3,5},{4,2},{5,3},{6,0},{7,1},{8,14},{9,15},{10,... | collective-permute-start | bytes 786440 | tf_op jit(solution)/shard_map/ppermute | solution.py:160
  120.1 3.6 %shard_map.91.refs_5_ = bf16[128,16384]{1,0:T(8,128)(2,1)} custom-call(s32[2]{0:T(128)} %pad_add_fusion.place_ref, bf16[128,1024]{1,0:T(8,128)(2,1)} %get-tuple-element.114.refs_0_, bf16[128,1024]{1,0:T(8,128)(2,1)} %copy-done.10, bf16[128,1024]{1,0:T(8,128)(2,1)} %copy-done.8, bf16[128,1024]{1,0:T(8,128)(2,1)} %copy-done.11, bf16[128,1024]{1,0:T(8,128)(2,1)} %copy-done.9, ...), custom_call_target="tpu_custom_call" | custom-call | bytes 4194304 | tf_op jit(solution)/shard_map/pallas_call | solution.py:296
  129.1 4.1 %collective-permute-done.39.refs_4_ = bf16[128,1024]{1,0:T(8,128)(2,1)S(1)} collective-permute-done((bf16[128,1024]{1,0:T(8,128)(2,1)S(1)}, bf16[128,1024]{1,0:T(8,128)(2,1)S(1)}, u32[]{:S(2)}, u32[]{:S(2)}) %collective-permute-start.39) | collective-permute-done | bytes 262176 | tf_op jit(solution)/shard_map/ppermute | solution.py:160
  133.9 3.0 %shard_map.92.refs_3_ = bf16[128,16384]{1,0:T(8,128)(2,1)} custom-call(s32[2]{0:T(128)} %pad_add_fusion.place_ref, bf16[128,1024]{1,0:T(8,128)(2,1)} %get-tuple-element.106.refs_0_, bf16[128,1024]{1,0:T(8,128)(2,1)} %copy-done.13, bf16[128,1024]{1,0:T(8,128)(2,1)} %copy-done.14, bf16[128,1024]{1,0:T(8,128)(2,1)} %copy-done.18, ...), custom_call_target="tpu_custom_call", output_to_operand_aliasing={{}: (6, {})} | custom-call | bytes 2621440 | tf_op jit(solution)/shard_map/pallas_call | solution.py:296
  137.0 1.9 %collective-permute-done.33.refs_1_ = bf16[128,1024]{1,0:T(8,128)(2,1)S(1)} collective-permute-done((bf16[128,1024]{1,0:T(8,128)(2,1)S(1)}, bf16[128,1024]{1,0:T(8,128)(2,1)S(1)}, u32[]{:S(2)}, u32[]{:S(2)}) %collective-permute-start.33) | collective-permute-done | bytes 262176 | tf_op jit(solution)/shard_map/ppermute | solution.py:160
  139.5 2.7 %shard_map.93 = bf16[128,16384]{1,0:T(8,128)(2,1)} custom-call(s32[2]{0:T(128)} %pad_add_fusion.place_ref, bf16[128,1024]{1,0:T(8,128)(2,1)} %copy-done.19, bf16[128,1024]{1,0:T(8,128)(2,1)} %copy-done.20, bf16[128,1024]{1,0:T(8,128)(2,1)} %copy-done.15, bf16[128,16384]{1,0:T(8,128)(2,1)} %shard_map.92.refs_3_), custom_call_target="tpu_custom_call", output_to_operand_aliasing={{}: (4, {})} | custom-call | bytes 1572864 | tf_op jit(solution)/shard_map/pallas_call | solution.py:296
  (152 shorter events, 41.1 us)
Async XLA Ops:
  8.0 17.5 %collective-permute-start.10 = (bf16[128,1024]{1,0:T(8,128)(2,1)}, bf16[128,1024]{1,0:T(8,128)(2,1)}, u32[]{:S(2)}, u32[]{:S(2)}) collective-permute-start(bf16[128,1024]{1,0:T(8,128)(2,1)} %constant_dynamic-slice_fusion.15), channel_id=1, source_target_pairs={{0,6},{1,7},{2,4},{3,5},{4,2},{5,3},{6,0},{7,1},{8,14},{9,15},{10,... | collective-permute-start | bytes 786440 | tf_op jit(solution)/shard_map/ppermute | solution.py:160
  9.4 22.1 %collective-permute-start.1 = (bf16[128,1024]{1,0:T(8,128)(2,1)}, bf16[128,1024]{1,0:T(8,128)(2,1)}, u32[]{:S(2)}, u32[]{:S(2)}) collective-permute-start(bf16[128,1024]{1,0:T(8,128)(2,1)} %constant_dynamic-slice_fusion.16), channel_id=1, source_target_pairs={{0,4},{1,5},{2,6},{3,7},{4,0},{5,1},{6,2},{7,3},{8,12},{9,13},{10,... | collective-permute-start | bytes 786440 | tf_op jit(solution)/shard_map/ppermute | solution.py:160
  25.5 28.6 %collective-permute-start.11 = (bf16[2,128,768]{2,1,0:T(8,128)(2,1)S(1)}, bf16[2,128,768]{2,1,0:T(8,128)(2,1)S(1)}, u32[]{:S(2)}, u32[]{:S(2)}) collective-permute-start(bf16[2,128,768]{2,1,0:T(8,128)(2,1)S(1)} %get-tuple-element.73), channel_id=1, source_target_pairs={{0,2},{1,3},{2,0},{3,1},{4,6},{5,7},{6,4},{7,5},{8,10},{9,11},{10,... | collective-permute-start | bytes 1179656 | tf_op jit(solution)/shard_map/ppermute | solution.py:160
  28.1 26.2 %collective-permute-start.15 = (bf16[2,128,768]{2,1,0:T(8,128)(2,1)S(1)}, bf16[2,128,768]{2,1,0:T(8,128)(2,1)S(1)}, u32[]{:S(2)}, u32[]{:S(2)}) collective-permute-start(bf16[2,128,768]{2,1,0:T(8,128)(2,1)S(1)} %get-tuple-element.76), channel_id=1, source_target_pairs={{0,4},{1,5},{2,6},{3,7},{4,0},{5,1},{6,2},{7,3},{8,12},{9,13},{10,... | collective-permute-start | bytes 1179656 | tf_op jit(solution)/shard_map/ppermute | solution.py:160
  30.5 24.1 %collective-permute-start.8 = (bf16[2,128,768]{2,1,0:T(8,128)(2,1)S(1)}, bf16[2,128,768]{2,1,0:T(8,128)(2,1)S(1)}, u32[]{:S(2)}, u32[]{:S(2)}) collective-permute-start(bf16[2,128,768]{2,1,0:T(8,128)(2,1)S(1)} %get-tuple-element.70), channel_id=1, source_target_pairs={{0,6},{1,7},{2,4},{3,5},{4,2},{5,3},{6,0},{7,1},{8,14},{9,15},{10,... | collective-permute-start | bytes 1179656 | tf_op jit(solution)/shard_map/ppermute | solution.py:160
  31.6 22.5 %collective-permute-start.2 = (bf16[128,1024]{1,0:T(8,128)(2,1)}, bf16[128,1024]{1,0:T(8,128)(2,1)}, u32[]{:S(2)}, u32[]{:S(2)}) collective-permute-start(bf16[128,1024]{1,0:T(8,128)(2,1)} %get-tuple-element.65), channel_id=1, source_target_pairs={{0,7},{1,6},{2,5},{3,4},{4,3},{5,2},{6,1},{7,0},{8,15},{9,14},{10,... | collective-permute-start | bytes 786440 | tf_op jit(solution)/shard_map/ppermute | solution.py:160
  38.8 16.0 %collective-permute-start.18 = (bf16[2,128,768]{2,1,0:T(8,128)(2,1)S(1)}, bf16[2,128,768]{2,1,0:T(8,128)(2,1)S(1)}, u32[]{:S(2)}, u32[]{:S(2)}) collective-permute-start(bf16[2,128,768]{2,1,0:T(8,128)(2,1)S(1)} %get-tuple-element.79.refs_0_), channel_id=1, source_target_pairs={{0,1},{1,0},{2,3},{3,2},{4,5},{5,4},{6,7},{7,6},{8,9},{9,8},{10,11... | collective-permute-start | bytes 1179656 | tf_op jit(solution)/shard_map/ppermute | solution.py:159
  54.3 11.3 %collective-permute-start.20 = (bf16[2,128,768]{2,1,0:T(8,128)(2,1)S(1)}, bf16[2,128,768]{2,1,0:T(8,128)(2,1)S(1)}, u32[]{:S(2)}, u32[]{:S(2)}) collective-permute-start(bf16[2,128,768]{2,1,0:T(8,128)(2,1)S(1)} %collective-permute-done.15.refs_4_), channel_id=1, source_target_pairs={{0,1},{1,0},{2,3},{3,2},{4,5},{5,4},{6,7},{7,6},{8,9},{9,8},{10,11... | collective-permute-start | bytes 1179656 | tf_op jit(solution)/shard_map/ppermute | solution.py:159
  54.6 12.2 %collective-permute-start.21 = (bf16[2,128,768]{2,1,0:T(8,128)(2,1)S(1)}, bf16[2,128,768]{2,1,0:T(8,128)(2,1)S(1)}, u32[]{:S(2)}, u32[]{:S(2)}) collective-permute-start(bf16[2,128,768]{2,1,0:T(8,128)(2,1)S(1)} %collective-permute-done.8.refs_6_), channel_id=1, source_target_pairs={{0,1},{1,0},{2,3},{3,2},{4,5},{5,4},{6,7},{7,6},{8,9},{9,8},{10,11... | collective-permute-start | bytes 1179656 | tf_op jit(solution)/shard_map/ppermute | solution.py:159
  63.6 18.8 %collective-permute-start.9 = (bf16[128,1024]{1,0:T(8,128)(2,1)}, bf16[128,1024]{1,0:T(8,128)(2,1)}, u32[]{:S(2)}, u32[]{:S(2)}) collective-permute-start(bf16[128,1024]{1,0:T(8,128)(2,1)} %get-tuple-element.71), channel_id=1, source_target_pairs={{0,3},{1,2},{2,1},{3,0},{4,7},{5,6},{6,5},{7,4},{8,11},{9,10},{10,... | collective-permute-start | bytes 786440 | tf_op jit(solution)/shard_map/ppermute | solution.py:160
  64.8 19.7 %collective-permute-start.13 = (bf16[128,1024]{1,0:T(8,128)(2,1)}, bf16[128,1024]{1,0:T(8,128)(2,1)}, u32[]{:S(2)}, u32[]{:S(2)}) collective-permute-start(bf16[128,1024]{1,0:T(8,128)(2,1)} %get-tuple-element.75), channel_id=1, source_target_pairs={{0,5},{1,4},{2,7},{3,6},{4,1},{5,0},{6,3},{7,2},{8,13},{9,12},{10,... | collective-permute-start | bytes 786440 | tf_op jit(solution)/shard_map/ppermute | solution.py:160
  65.5 19.0 %collective-permute-start.16 = (bf16[128,1024]{1,0:T(8,128)(2,1)S(1)}, bf16[128,1024]{1,0:T(8,128)(2,1)}, u32[]{:S(2)}, u32[]{:S(2)}) collective-permute-start(bf16[128,1024]{1,0:T(8,128)(2,1)S(1)} %get-tuple-element.77), channel_id=1, source_target_pairs={{0,6},{1,7},{2,4},{3,5},{4,2},{5,3},{6,0},{7,1},{8,14},{9,15},{10,... | collective-permute-start | bytes 786440 | tf_op jit(solution)/shard_map/ppermute | solution.py:160
  66.8 17.7 %collective-permute-start.17 = (bf16[128,1024]{1,0:T(8,128)(2,1)S(1)}, bf16[128,1024]{1,0:T(8,128)(2,1)}, u32[]{:S(2)}, u32[]{:S(2)}) collective-permute-start(bf16[128,1024]{1,0:T(8,128)(2,1)S(1)} %get-tuple-element.78), channel_id=1, source_target_pairs={{0,7},{1,6},{2,5},{3,4},{4,3},{5,2},{6,1},{7,0},{8,15},{9,14},{10,... | collective-permute-start | bytes 786440 | tf_op jit(solution)/shard_map/ppermute | solution.py:160
  84.5 21.1 %collective-permute-start.35 = (bf16[128,1024]{1,0:T(8,128)(2,1)}, bf16[128,1024]{1,0:T(8,128)(2,1)S(1)}, u32[]{:S(2)}, u32[]{:S(2)}) collective-permute-start(bf16[128,1024]{1,0:T(8,128)(2,1)} %get-tuple-element.109), channel_id=1, source_target_pairs={{0,3},{1,2},{2,1},{3,0},{4,7},{5,6},{6,5},{7,4},{8,11},{9,10},{10,... | collective-permute-start | bytes 786440 | tf_op jit(solution)/shard_map/ppermute | solution.py:160
  85.2 18.4 %collective-permute-start.26 = (bf16[128,1024]{1,0:T(8,128)(2,1)}, bf16[128,1024]{1,0:T(8,128)(2,1)S(1)}, u32[]{:S(2)}, u32[]{:S(2)}) collective-permute-start(bf16[128,1024]{1,0:T(8,128)(2,1)} %get-tuple-element.93), channel_id=1, source_target_pairs={{0,2},{1,3},{2,0},{3,1},{4,6},{5,7},{6,4},{7,5},{8,10},{9,11},{10,... | collective-permute-start | bytes 786440 | tf_op jit(solution)/shard_map/ppermute | solution.py:160
  86.4 21.0 %collective-permute-start.24 = (bf16[128,1024]{1,0:T(8,128)(2,1)}, bf16[128,1024]{1,0:T(8,128)(2,1)S(1)}, u32[]{:S(2)}, u32[]{:S(2)}) collective-permute-start(bf16[128,1024]{1,0:T(8,128)(2,1)} %get-tuple-element.89), channel_id=1, source_target_pairs={{0,6},{1,7},{2,4},{3,5},{4,2},{5,3},{6,0},{7,1},{8,14},{9,15},{10,... | collective-permute-start | bytes 786440 | tf_op jit(solution)/shard_map/ppermute | solution.py:160
  91.5 17.9 %collective-permute-start.31 = (bf16[128,1024]{1,0:T(8,128)(2,1)}, bf16[128,1024]{1,0:T(8,128)(2,1)S(1)}, u32[]{:S(2)}, u32[]{:S(2)}) collective-permute-start(bf16[128,1024]{1,0:T(8,128)(2,1)} %get-tuple-element.102), channel_id=1, source_target_pairs={{0,7},{1,6},{2,5},{3,4},{4,3},{5,2},{6,1},{7,0},{8,15},{9,14},{10,... | collective-permute-start | bytes 786440 | tf_op jit(solution)/shard_map/ppermute | solution.py:160
  103.6 14.4 %collective-permute-start.38 = (bf16[128,1024]{1,0:T(8,128)(2,1)S(1)}, bf16[128,1024]{1,0:T(8,128)(2,1)S(1)}, u32[]{:S(2)}, u32[]{:S(2)}) collective-permute-start(bf16[128,1024]{1,0:T(8,128)(2,1)S(1)} %copy-done.29), channel_id=1, source_target_pairs={{0,1},{1,0},{2,3},{3,2},{4,5},{5,4},{6,7},{7,6},{8,9},{9,8},{10,11... | collective-permute-start | bytes 786440 | tf_op jit(solution)/shard_map/ppermute | solution.py:159
  104.5 12.5 %collective-permute-start.27 = (bf16[128,1024]{1,0:T(8,128)(2,1)S(1)}, bf16[128,1024]{1,0:T(8,128)(2,1)S(1)}, u32[]{:S(2)}, u32[]{:S(2)}) collective-permute-start(bf16[128,1024]{1,0:T(8,128)(2,1)S(1)} %copy-done.31), channel_id=1, source_target_pairs={{0,5},{1,4},{2,7},{3,6},{4,1},{5,0},{6,3},{7,2},{8,13},{9,12},{10,... | collective-permute-start | bytes 786440 | tf_op jit(solution)/shard_map/ppermute | solution.py:160
  105.6 18.1 %collective-permute-start.36 = (bf16[128,1024]{1,0:T(8,128)(2,1)}, bf16[128,1024]{1,0:T(8,128)(2,1)S(1)}, u32[]{:S(2)}, u32[]{:S(2)}) collective-permute-start(bf16[128,1024]{1,0:T(8,128)(2,1)} %get-tuple-element.110), channel_id=1, source_target_pairs={{0,2},{1,3},{2,0},{3,1},{4,6},{5,7},{6,4},{7,5},{8,10},{9,11},{10,... | collective-permute-start | bytes 786440 | tf_op jit(solution)/shard_map/ppermute | solution.py:160
  109.4 15.8 %collective-permute-start.32 = (bf16[128,1024]{1,0:T(8,128)(2,1)}, bf16[128,1024]{1,0:T(8,128)(2,1)S(1)}, u32[]{:S(2)}, u32[]{:S(2)}) collective-permute-start(bf16[128,1024]{1,0:T(8,128)(2,1)} %get-tuple-element.103), channel_id=1, source_target_pairs={{0,4},{1,5},{2,6},{3,7},{4,0},{5,1},{6,2},{7,3},{8,12},{9,13},{10,... | collective-permute-start | bytes 786440 | tf_op jit(solution)/shard_map/ppermute | solution.py:160
  118.0 18.9 %collective-permute-start.34 = (bf16[128,1024]{1,0:T(8,128)(2,1)}, bf16[128,1024]{1,0:T(8,128)(2,1)S(1)}, u32[]{:S(2)}, u32[]{:S(2)}) collective-permute-start(bf16[128,1024]{1,0:T(8,128)(2,1)} %get-tuple-element.105), channel_id=1, source_target_pairs={{0,1},{1,0},{2,3},{3,2},{4,5},{5,4},{6,7},{7,6},{8,9},{9,8},{10,11... | collective-permute-start | bytes 786440 | tf_op jit(solution)/shard_map/ppermute | solution.py:159
  124.7 12.3 %collective-permute-start.29 = (bf16[128,1024]{1,0:T(8,128)(2,1)S(1)}, bf16[128,1024]{1,0:T(8,128)(2,1)S(1)}, u32[]{:S(2)}, u32[]{:S(2)}) collective-permute-start(bf16[128,1024]{1,0:T(8,128)(2,1)S(1)} %copy-done.28), channel_id=1, source_target_pairs={{0,5},{1,4},{2,7},{3,6},{4,1},{5,0},{6,3},{7,2},{8,13},{9,12},{10,... | collective-permute-start | bytes 786440 | tf_op jit(solution)/shard_map/ppermute | solution.py:160
  125.2 13.7 %collective-permute-start.33 = (bf16[128,1024]{1,0:T(8,128)(2,1)S(1)}, bf16[128,1024]{1,0:T(8,128)(2,1)S(1)}, u32[]{:S(2)}, u32[]{:S(2)}) collective-permute-start(bf16[128,1024]{1,0:T(8,128)(2,1)S(1)} %copy-done.27), channel_id=1, source_target_pairs={{0,7},{1,6},{2,5},{3,4},{4,3},{5,2},{6,1},{7,0},{8,15},{9,14},{10,... | collective-permute-start | bytes 786440 | tf_op jit(solution)/shard_map/ppermute | solution.py:160
  (50 other events, 455.4 us)

commit v2 on v1

--- a/solution.py
+++ b/solution.py
@@ -13,7 +13,7 @@
 PAD_ROWS = 16
 VMEM_BYTES = 60 * 1024 * 1024
 IN_FLIGHT = 4
-FIRST = 3
+FIRST = 4
 EARLY = 3
 ASSEMBLE_BEFORE = 4
 
@@ -153,7 +153,9 @@
             x, sent[-IN_FLIGHT] = lax.optimization_barrier((x, sent[-IN_FLIGHT]))
         return x
 
-    def partner(x, flip):
+    def partner(x, flip, after=()):
+        if after:
+            x = lax.optimization_barrier((x, *after))[0]
         pairs = [(i, i ^ flip) for i in range(count)]
         if flip == 1:
             return lax.ppermute(x, "mem", pairs)
@@ -220,7 +222,8 @@
     for chunk in range(1, CHUNKS):
         for flip in order:
             if flip not in got[chunk]:
-                got[chunk][flip] = partner(outgoing(source, flip, chunk), flip)
+                after = [pieces[flip - 2]] if chunk == 1 and flip & 1 and flip > 1 else []
+                got[chunk][flip] = partner(outgoing(source, flip, chunk), flip, after)
     priors = [[pieces_of[i] for i in range(1, count)] for pieces_of in got]
 
     ydt, solved, ysum = pl.pallas_call(
@@ -241,9 +244,6 @@
             jax.ShapeDtypeStruct((width, span), jnp.float32),
         ],
         compiler_params=pltpu.CompilerParams(vmem_limit_bytes=VMEM_BYTES),
-        cost_estimate=pl.CostEstimate(
-            flops=20 * members * width, bytes_accessed=8 * members * width, transcendentals=0
-        ),
     )(place, *pieces)
 
     step_span = STEP_PATCHES * span
@@ -283,11 +283,6 @@
             out_shape=[jax.ShapeDtypeStruct((rows, chunk_span), jnp.bfloat16)] * count
             + [jax.ShapeDtypeStruct((chunk_patches, span), jnp.float32)],
             compiler_params=pltpu.CompilerParams(vmem_limit_bytes=VMEM_BYTES),
-            cost_estimate=pl.CostEstimate(
-                flops=4 * members * width * chunk_span,
-                bytes_accessed=4 * members * (width + chunk_span),
-                transcendentals=0,
-            ),
         )(place, blocks, tapers, prior_ensemble, *prior, ydt, solved, ysum, taper)
         return out, variance
 
@@ -306,9 +301,6 @@
             out_shape=jax.ShapeDtypeStruct(prior_ensemble.shape, prior_ensemble.dtype),
             input_output_aliases={1 + len(pieces): 0} if base else {},
             compiler_params=pltpu.CompilerParams(vmem_limit_bytes=VMEM_BYTES),
-            cost_estimate=pl.CostEstimate(
-                flops=0, bytes_accessed=4 * len(pieces) * rows * chunk_span, transcendentals=0
-            ),
         )(place, *pieces, *base)
 
     analysis = None

time: 143 us -> 140 us (0.979)
  starting transfers between devices: 44.6 us -> 35.4 us
  waiting for transfers between devices: 41.4 us -> 45 us
  local copies, waits for them, and re-layouts: 11.8 us -> 14.2 us
    ppermute x29, starting transfers between devices: 36.4 us -> 29.1 us  [partner(): sent.append(lax.ppermute(after_sent(x), 'mem', pairs))]
    ppermute x1, waiting for transfers between devices: 1.56 us -> 4.74 us  [per_device(): after = lax.ppermute(both[:, :, :rim], 'band', down)]
    ppermute x9, starting transfers between devices: 3.23 us -> 1.5 us  [partner(): return lax.ppermute(x, 'mem', pairs)]
    dynamic_slice x4 -> x5, local copies, waits for them, and re-layouts: 7.36 us -> 9.06 us  [outgoing(): return lax.dynamic_slice_in_dim(source, first, chunk_span, 1)]
    unnamed x74 -> x82, local copies, waits for them, and re-layouts: 4.29 us -> 4.99 us
  transfers between devices with their start and end apart: 40 -> 40, of which waited for: 11 -> 15; matrix products, arithmetic and copies ran while one was open for 8% -> 9% of each run, Pallas kernels for 26% -> 27%
where the time goes in v2:
time: 140 us; the launch traced here: 139 us
  waiting for transfers between devices  45 us (32%)
  Pallas kernels  39.8 us (28%)
  starting transfers between devices  35.4 us (25%)
  local copies, waits for them, and re-layouts  14.2 us (10%)
  other arithmetic  3.88 us (3%)
    ppermute x29, waiting for transfers between devices, partner(): sent.append(lax.ppermute(after_sent(x), 'mem', pairs))  39.5 us
    ppermute x29, starting transfers between devices, partner(): sent.append(lax.ppermute(after_sent(x), 'mem', pairs))  29.1 us
    pallas_call x2, Pallas kernels, analyse(): pl.pallas_call(functools.partial(analyse_kernel, count, rows, span, obs_l...  18.6 us
    pallas_call x3, Pallas kernels, assemble(): pl.pallas_call(functools.partial(assemble_kernel, moves, span), grid_spec...  9.23 us
    dynamic_slice x5, local copies, waits for them, and re-layouts, outgoing(): return lax.dynamic_slice_in_dim(source, first, chunk_span, 1)  9.06 us
    unnamed x82, local copies, waits for them, and re-layouts  4.99 us
    pallas_call x1, Pallas kernels, per_device(): pl.pallas_call(functools.partial(prepare_kernel, count, rows, width, cent...  4.99 us
    ppermute x1, waiting for transfers between devices, per_device(): after = lax.ppermute(both[:, :, :rim], 'band', down)  4.74 us
  transfers between devices with their start and end apart: 40, of which 15 were waited for; matrix products, arithmetic and copies ran while one was open for 9% of the time, Pallas kernels for 27%

profile of v2, /device:TPU:0, one launch (start us, length us, event | category | flops | bytes accessed | tf_op | source)
XLA Modules:
  0.0 139.3 jit_solution(1317750791120621789)
XLA Ops:
  1.6 3.0 %collective-permute-start.4 = (bf16[128,1024]{1,0:T(8,128)(2,1)S(1)}, bf16[128,1024]{1,0:T(8,128)(2,1)S(1)}, u32[]{:S(2)}, u32[]{:S(2)}) collective-permute-start(bf16[128,1024]{1,0:T(8,128)(2,1)S(1)} %constant_dynamic-slice_fusion.17), channel_id=1, source_target_pairs={{0,2},{1,3},{2,0},{3,1},{4,6},{5,7},{6,4},{7,5},{8,10},{9,11},{10,... | collective-permute-start | bytes 786440 | tf_op jit(solution)/shard_map/ppermute | solution.py:162
  9.6 2.1 %collective-permute-start.11 = (bf16[128,1024]{1,0:T(8,128)(2,1)}, bf16[128,1024]{1,0:T(8,128)(2,1)S(1)}, u32[]{:S(2)}, u32[]{:S(2)}) collective-permute-start(bf16[128,1024]{1,0:T(8,128)(2,1)} %constant_dynamic-slice_fusion.15), channel_id=1, source_target_pairs={{0,6},{1,7},{2,4},{3,5},{4,2},{5,3},{6,0},{7,1},{8,14},{9,15},{10,... | collective-permute-start | bytes 786440 | tf_op jit(solution)/shard_map/ppermute | solution.py:162
  13.4 3.5 %collective-permute-start.5 = (bf16[2,128,256]{2,1,0:T(8,128)(2,1)S(1)}, bf16[2,128,256]{2,1,0:T(8,128)(2,1)S(1)}, u32[]{:S(2)}, u32[]{:S(2)}) collective-permute-start(bf16[2,128,256]{2,1,0:T(8,128)(2,1)S(1)} %get-tuple-element.145), channel_id=1, source_target_pairs={{0,8},{8,16},{16,24},{1,9},{9,17},{17,25},{2,10},{10,18},{18,26},{... | collective-permute-start | bytes 393224 | tf_op jit(solution)/shard_map/ppermute | solution.py:203
  16.9 3.1 %constant_dynamic-slice_fusion = (bf16[128,1024]{1,0:T(8,128)(2,1)}, bf16[128,1024]{1,0:T(8,128)(2,1)}, bf16[128,1024]{1,0:T(8,128)(2,1)}, bf16[128,1024]{1,0:T(...) fusion(bf16[128,16384]{1,0:T(8,128)(2,1)} %refs_0_.3, ...), kind=kLoop, calls=%fused_computation.12 | loop fusion | bytes 5242920 | tf_op jit(solution)/shard_map/dynamic_slice | solution.py:190
  22.7 4.7 %collective-permute-done.6 = bf16[2,128,256]{2,1,0:T(8,128)(2,1)S(1)} collective-permute-done((bf16[2,128,256]{2,1,0:T(8,128)(2,1)S(1)}, bf16[2,128,256]{2,1,0:T(8,128)(2,1)S(1)}, u32[]{:S(2)}, u32[]{:S(2)}) %collective-permute-start.6) | collective-permute-done | bytes 131104 | tf_op jit(solution)/shard_map/ppermute | solution.py:204
  29.7 2.1 %collective-permute-done.8.refs_5_ = bf16[128,1024]{1,0:T(8,128)(2,1)S(1)} collective-permute-done((bf16[128,1024]{1,0:T(8,128)(2,1)S(1)}, bf16[128,1024]{1,0:T(8,128)(2,1)S(1)}, u32[]{:S(2)}, u32[]{:S(2)}) %collective-permute-start.8) | collective-permute-done | bytes 262176 | tf_op jit(solution)/shard_map/ppermute | solution.py:162
  32.9 2.1 %shard_map.87.refs_11_ = f32[8,128,128]{2,1,0:T(8,128)} custom-call(f32[8,128,128]{2,1,0:T(8,128)} %loc_ref.1), custom_call_target="tpu_custom_call" | custom-call | tf_op jit(solution)/shard_map/pallas_call | solution.py:180
  35.6 3.4 %shard_map.86.select_ref = f32[32,128]{1,0:T(8,128)} custom-call(s32[128]{0:T(128)} %owner_ref.1, s32[2]{0:T(128)} %pad_add_fusion.place_ref), custom_call_target="tpu_custom_call" | custom-call | tf_op jit(solution)/shard_map/pallas_call | solution.py:170
  39.7 3.8 %collective-permute-done.2.refs_7_ = bf16[128,1024]{1,0:T(8,128)(2,1)} collective-permute-done((bf16[128,1024]{1,0:T(8,128)(2,1)}, bf16[128,1024]{1,0:T(8,128)(2,1)}, u32[]{:S(2)}, u32[]{:S(2)}) %collective-permute-start.2) | collective-permute-done | bytes 262176 | tf_op jit(solution)/shard_map/ppermute | solution.py:162
  45.0 9.3 %collective-permute-done.17.refs_4_ = bf16[2,128,768]{2,1,0:T(8,128)(2,1)S(1)} collective-permute-done((bf16[2,128,768]{2,1,0:T(8,128)(2,1)S(1)}, bf16[2,128,768]{2,1,0:T(8,128)(2,1)S(1)}, u32[]{:S(2)}, u32[]{:S(2)}) %collective-permute-start.17) | collective-permute-done | bytes 393248 | tf_op jit(solution)/shard_map/ppermute | solution.py:162
  55.4 2.3 %collective-permute-done.3.refs_2_ = bf16[128,1024]{1,0:T(8,128)(2,1)S(1)} collective-permute-done((bf16[128,1024]{1,0:T(8,128)(2,1)}, bf16[128,1024]{1,0:T(8,128)(2,1)S(1)}, u32[]{:S(2)}, u32[]{:S(2)}) %collective-permute-start.3) | collective-permute-done | bytes 262176 | tf_op jit(solution)/shard_map/ppermute | solution.py:162
  58.1 2.7 %collective-permute-start.18 = (bf16[128,1024]{1,0:T(8,128)(2,1)}, bf16[128,1024]{1,0:T(8,128)(2,1)}, u32[]{:S(2)}, u32[]{:S(2)}) collective-permute-start(bf16[128,1024]{1,0:T(8,128)(2,1)} %get-tuple-element.87), channel_id=1, source_target_pairs={{0,6},{1,7},{2,4},{3,5},{4,2},{5,3},{6,0},{7,1},{8,14},{9,15},{10,... | collective-permute-start | bytes 786440 | tf_op jit(solution)/shard_map/ppermute | solution.py:162
  60.8 2.9 %collective-permute-done.13.refs_4_ = bf16[128,1024]{1,0:T(8,128)(2,1)S(1)} collective-permute-done((bf16[128,1024]{1,0:T(8,128)(2,1)}, bf16[128,1024]{1,0:T(8,128)(2,1)S(1)}, u32[]{:S(2)}, u32[]{:S(2)}) %collective-permute-start.13) | collective-permute-done | bytes 262176 | tf_op jit(solution)/shard_map/ppermute | solution.py:162
  65.5 5.0 %shard_map.88 = (bf16[656,1024]{1,0:T(8,128)(2,1)}, bf16[1024,640]{1,0:T(8,128)(2,1)}, f32[640,128]{1,0:T(8,128)}) custom-call(s32[2]{0:T(128)} %pad_add_fusion.place_ref, bf16[2,128,768]{2,1,0:T(8,128)(2,1)} %copy-done, bf16[2,128,768]{2,1,0:T(8,128)(2,1)} %copy-done.4, bf16[2,128,768]{2,1,0:T(8,128)(2,1)} %copy-done.1, bf16[2,128,768]{2,1,0:T(8,128)(2,1)} %copy-done.5, ...), custom_call_target="tpu_custom_call" | custom-call | tf_op jit(solution)/shard_map/pallas_call | solution.py:229
  70.5 9.4 %shard_map.90 = (bf16[128,1024]{1,0:T(8,128)(2,1)}, bf16[128,1024]{1,0:T(8,128)(2,1)}, bf16[128,1024]{1,0:T(8,128)(2,1)}, bf16[128,1024]{1,0:T(8,128)(2,1)}, bf1...) custom-call(s32[2]{0:T(128)} %pad_add_fusion.place_ref, ...), custom_call_target="tpu_custom_call" | custom-call | tf_op jit(solution)/shard_map/pallas_call | solution.py:259
  84.8 4.4 %collective-permute-done.30.refs_2_ = bf16[128,1024]{1,0:T(8,128)(2,1)S(1)} collective-permute-done((bf16[128,1024]{1,0:T(8,128)(2,1)}, bf16[128,1024]{1,0:T(8,128)(2,1)S(1)}, u32[]{:S(2)}, u32[]{:S(2)}) %collective-permute-start.30) | collective-permute-done | bytes 262176 | tf_op jit(solution)/shard_map/ppermute | solution.py:162
  90.5 9.2 %shard_map.89 = (bf16[128,1024]{1,0:T(8,128)(2,1)}, bf16[128,1024]{1,0:T(8,128)(2,1)}, bf16[128,1024]{1,0:T(8,128)(2,1)}, bf16[128,1024]{1,0:T(8,128)(2,1)}, bf1...) custom-call(s32[2]{0:T(128)} %pad_add_fusion.place_ref, ...), custom_call_target="tpu_custom_call" | custom-call | tf_op jit(solution)/shard_map/pallas_call | solution.py:259
  107.5 5.1 %collective-permute-done.25 = f32[32,128]{1,0:T(8,128)S(1)} collective-permute-done((f32[32,128]{1,0:T(8,128)S(1)}, f32[32,128]{1,0:T(8,128)S(1)}, u32[]{:S(2)}, u32[]{:S(2)}) %collective-permute-start.25) | collective-permute-done | bytes 16416 | tf_op jit(solution)/shard_map/ppermute | solution.py:162
  115.2 1.8 %collective-permute-start.37 = (bf16[128,1024]{1,0:T(8,128)(2,1)}, bf16[128,1024]{1,0:T(8,128)(2,1)S(1)}, u32[]{:S(2)}, u32[]{:S(2)}) collective-permute-start(bf16[128,1024]{1,0:T(8,128)(2,1)} %get-tuple-element.122), channel_id=1, source_target_pairs={{0,6},{1,7},{2,4},{3,5},{4,2},{5,3},{6,0},{7,1},{8,14},{9,15},{10,... | collective-permute-start | bytes 786440 | tf_op jit(solution)/shard_map/ppermute | solution.py:162
  117.0 3.5 %shard_map.91.refs_5_ = bf16[128,16384]{1,0:T(8,128)(2,1)} custom-call(s32[2]{0:T(128)} %pad_add_fusion.place_ref, bf16[128,1024]{1,0:T(8,128)(2,1)} %get-tuple-element.124.refs_0_, bf16[128,1024]{1,0:T(8,128)(2,1)} %copy-done.17, bf16[128,1024]{1,0:T(8,128)(2,1)} %copy-done.15, bf16[128,1024]{1,0:T(8,128)(2,1)} %copy-done.19, bf16[128,1024]{1,0:T(8,128)(2,1)} %copy-done.18, ...), custom_call_target="tpu_custom_call" | custom-call | tf_op jit(solution)/shard_map/pallas_call | solution.py:291
  126.0 3.9 %collective-permute-done.39.refs_4_ = bf16[128,1024]{1,0:T(8,128)(2,1)S(1)} collective-permute-done((bf16[128,1024]{1,0:T(8,128)(2,1)S(1)}, bf16[128,1024]{1,0:T(8,128)(2,1)S(1)}, u32[]{:S(2)}, u32[]{:S(2)}) %collective-permute-start.39) | collective-permute-done | bytes 262176 | tf_op jit(solution)/shard_map/ppermute | solution.py:162
  130.6 3.0 %shard_map.92.refs_3_ = bf16[128,16384]{1,0:T(8,128)(2,1)} custom-call(s32[2]{0:T(128)} %pad_add_fusion.place_ref, bf16[128,1024]{1,0:T(8,128)(2,1)} %get-tuple-element.116.refs_0_, bf16[128,1024]{1,0:T(8,128)(2,1)} %copy-done.21, bf16[128,1024]{1,0:T(8,128)(2,1)} %copy-done.22, bf16[128,1024]{1,0:T(8,128)(2,1)} %copy-done.26, ...), custom_call_target="tpu_custom_call", output_to_operand_aliasing={{}: (6, {})} | custom-call | tf_op jit(solution)/shard_map/pallas_call | solution.py:291
  133.7 2.2 %collective-permute-done.33.refs_1_ = bf16[128,1024]{1,0:T(8,128)(2,1)S(1)} collective-permute-done((bf16[128,1024]{1,0:T(8,128)(2,1)S(1)}, bf16[128,1024]{1,0:T(8,128)(2,1)S(1)}, u32[]{:S(2)}, u32[]{:S(2)}) %collective-permute-start.33) | collective-permute-done | bytes 262176 | tf_op jit(solution)/shard_map/ppermute | solution.py:162
  136.6 2.7 %shard_map.93 = bf16[128,16384]{1,0:T(8,128)(2,1)} custom-call(s32[2]{0:T(128)} %pad_add_fusion.place_ref, bf16[128,1024]{1,0:T(8,128)(2,1)} %copy-done.27, bf16[128,1024]{1,0:T(8,128)(2,1)} %copy-done.29, bf16[128,1024]{1,0:T(8,128)(2,1)} %copy-done.23, bf16[128,16384]{1,0:T(8,128)(2,1)} %shard_map.92.refs_3_), custom_call_target="tpu_custom_call", output_to_operand_aliasing={{}: (4, {})} | custom-call | tf_op jit(solution)/shard_map/pallas_call | solution.py:291
  (161 shorter events, 43.2 us)
Async XLA Ops:
  9.6 18.5 %collective-permute-start.16 = (bf16[128,1024]{1,0:T(8,128)(2,1)}, bf16[128,1024]{1,0:T(8,128)(2,1)S(1)}, u32[]{:S(2)}, u32[]{:S(2)}) collective-permute-start(bf16[128,1024]{1,0:T(8,128)(2,1)} %constant_dynamic-slice_fusion.14), channel_id=1, source_target_pairs={{0,3},{1,2},{2,1},{3,0},{4,7},{5,6},{6,5},{7,4},{8,11},{9,10},{10,... | collective-permute-start | bytes 786440 | tf_op jit(solution)/shard_map/ppermute | solution.py:162
  9.6 18.0 %collective-permute-start.11 = (bf16[128,1024]{1,0:T(8,128)(2,1)}, bf16[128,1024]{1,0:T(8,128)(2,1)S(1)}, u32[]{:S(2)}, u32[]{:S(2)}) collective-permute-start(bf16[128,1024]{1,0:T(8,128)(2,1)} %constant_dynamic-slice_fusion.15), channel_id=1, source_target_pairs={{0,6},{1,7},{2,4},{3,5},{4,2},{5,3},{6,0},{7,1},{8,14},{9,15},{10,... | collective-permute-start | bytes 786440 | tf_op jit(solution)/shard_map/ppermute | solution.py:162
  11.8 17.9 %collective-permute-start.1 = (bf16[128,1024]{1,0:T(8,128)(2,1)}, bf16[128,1024]{1,0:T(8,128)(2,1)S(1)}, u32[]{:S(2)}, u32[]{:S(2)}) collective-permute-start(bf16[128,1024]{1,0:T(8,128)(2,1)} %constant_dynamic-slice_fusion.16), channel_id=1, source_target_pairs={{0,4},{1,5},{2,6},{3,7},{4,0},{5,1},{6,2},{7,3},{8,12},{9,13},{10,... | collective-permute-start | bytes 786440 | tf_op jit(solution)/shard_map/ppermute | solution.py:162
  28.2 26.2 %collective-permute-start.17 = (bf16[2,128,768]{2,1,0:T(8,128)(2,1)S(1)}, bf16[2,128,768]{2,1,0:T(8,128)(2,1)S(1)}, u32[]{:S(2)}, u32[]{:S(2)}) collective-permute-start(bf16[2,128,768]{2,1,0:T(8,128)(2,1)S(1)} %get-tuple-element.86), channel_id=1, source_target_pairs={{0,4},{1,5},{2,6},{3,7},{4,0},{5,1},{6,2},{7,3},{8,12},{9,13},{10,... | collective-permute-start | bytes 1179656 | tf_op jit(solution)/shard_map/ppermute | solution.py:162
  29.7 13.8 %collective-permute-start.2 = (bf16[128,1024]{1,0:T(8,128)(2,1)}, bf16[128,1024]{1,0:T(8,128)(2,1)}, u32[]{:S(2)}, u32[]{:S(2)}) collective-permute-start(bf16[128,1024]{1,0:T(8,128)(2,1)} %get-tuple-element.71), channel_id=1, source_target_pairs={{0,7},{1,6},{2,5},{3,4},{4,3},{5,2},{6,1},{7,0},{8,15},{9,14},{10,... | collective-permute-start | bytes 786440 | tf_op jit(solution)/shard_map/ppermute | solution.py:162
  32.5 22.2 %collective-permute-start.9 = (bf16[2,128,768]{2,1,0:T(8,128)(2,1)S(1)}, bf16[2,128,768]{2,1,0:T(8,128)(2,1)S(1)}, u32[]{:S(2)}, u32[]{:S(2)}) collective-permute-start(bf16[2,128,768]{2,1,0:T(8,128)(2,1)S(1)} %get-tuple-element.78), channel_id=1, source_target_pairs={{0,6},{1,7},{2,4},{3,5},{4,2},{5,3},{6,0},{7,1},{8,14},{9,15},{10,... | collective-permute-start | bytes 1179656 | tf_op jit(solution)/shard_map/ppermute | solution.py:162
  39.0 15.9 %collective-permute-start.7 = (bf16[2,128,768]{2,1,0:T(8,128)(2,1)S(1)}, bf16[2,128,768]{2,1,0:T(8,128)(2,1)S(1)}, u32[]{:S(2)}, u32[]{:S(2)}) collective-permute-start(bf16[2,128,768]{2,1,0:T(8,128)(2,1)S(1)} %get-tuple-element.75.refs_0_), channel_id=1, source_target_pairs={{0,1},{1,0},{2,3},{3,2},{4,5},{5,4},{6,7},{7,6},{8,9},{9,8},{10,11... | collective-permute-start | bytes 1179656 | tf_op jit(solution)/shard_map/ppermute | solution.py:161
  39.7 18.0 %collective-permute-start.14 = (bf16[2,128,768]{2,1,0:T(8,128)(2,1)S(1)}, bf16[2,128,768]{2,1,0:T(8,128)(2,1)S(1)}, u32[]{:S(2)}, u32[]{:S(2)}) collective-permute-start(bf16[2,128,768]{2,1,0:T(8,128)(2,1)S(1)} %collective-permute-done.12.refs_2_), channel_id=1, source_target_pairs={{0,1},{1,0},{2,3},{3,2},{4,5},{5,4},{6,7},{7,6},{8,9},{9,8},{10,11... | collective-permute-start | bytes 1179656 | tf_op jit(solution)/shard_map/ppermute | solution.py:161
  43.5 14.2 %collective-permute-start.3 = (bf16[128,1024]{1,0:T(8,128)(2,1)}, bf16[128,1024]{1,0:T(8,128)(2,1)S(1)}, u32[]{:S(2)}, u32[]{:S(2)}) collective-permute-start(bf16[128,1024]{1,0:T(8,128)(2,1)} %get-tuple-element.72), channel_id=1, source_target_pairs={{0,2},{1,3},{2,0},{3,1},{4,6},{5,7},{6,4},{7,5},{8,10},{9,11},{10,... | collective-permute-start | bytes 786440 | tf_op jit(solution)/shard_map/ppermute | solution.py:162
  57.7 12.8 %collective-permute-start.22 = (bf16[128,1024]{1,0:T(8,128)(2,1)}, bf16[128,1024]{1,0:T(8,128)(2,1)}, u32[]{:S(2)}, u32[]{:S(2)}) collective-permute-start(bf16[128,1024]{1,0:T(8,128)(2,1)} %get-tuple-element.130), channel_id=1, source_target_pairs={{0,1},{1,0},{2,3},{3,2},{4,5},{5,4},{6,7},{7,6},{8,9},{9,8},{10,11... | collective-permute-start | bytes 786440 | tf_op jit(solution)/shard_map/ppermute | solution.py:161
  57.7 22.2 %collective-permute-start.10 = (bf16[128,1024]{1,0:T(8,128)(2,1)}, bf16[128,1024]{1,0:T(8,128)(2,1)}, u32[]{:S(2)}, u32[]{:S(2)}) collective-permute-start(bf16[128,1024]{1,0:T(8,128)(2,1)} %get-tuple-element.79), channel_id=1, source_target_pairs={{0,3},{1,2},{2,1},{3,0},{4,7},{5,6},{6,5},{7,4},{8,11},{9,10},{10,... | collective-permute-start | bytes 786440 | tf_op jit(solution)/shard_map/ppermute | solution.py:162
  58.1 22.7 %collective-permute-start.18 = (bf16[128,1024]{1,0:T(8,128)(2,1)}, bf16[128,1024]{1,0:T(8,128)(2,1)}, u32[]{:S(2)}, u32[]{:S(2)}) collective-permute-start(bf16[128,1024]{1,0:T(8,128)(2,1)} %get-tuple-element.87), channel_id=1, source_target_pairs={{0,6},{1,7},{2,4},{3,5},{4,2},{5,3},{6,0},{7,1},{8,14},{9,15},{10,... | collective-permute-start | bytes 786440 | tf_op jit(solution)/shard_map/ppermute | solution.py:162
  63.7 20.0 %collective-permute-start.15 = (bf16[128,1024]{1,0:T(8,128)(2,1)}, bf16[128,1024]{1,0:T(8,128)(2,1)}, u32[]{:S(2)}, u32[]{:S(2)}) collective-permute-start(bf16[128,1024]{1,0:T(8,128)(2,1)} %get-tuple-element.84), channel_id=1, source_target_pairs={{0,5},{1,4},{2,7},{3,6},{4,1},{5,0},{6,3},{7,2},{8,13},{9,12},{10,... | collective-permute-start | bytes 786440 | tf_op jit(solution)/shard_map/ppermute | solution.py:162
  64.4 17.9 %collective-permute-start.20 = (bf16[128,1024]{1,0:T(8,128)(2,1)}, bf16[128,1024]{1,0:T(8,128)(2,1)}, u32[]{:S(2)}, u32[]{:S(2)}) collective-permute-start(bf16[128,1024]{1,0:T(8,128)(2,1)} %get-tuple-element.89), channel_id=1, source_target_pairs={{0,7},{1,6},{2,5},{3,4},{4,3},{5,2},{6,1},{7,0},{8,15},{9,14},{10,... | collective-permute-start | bytes 786440 | tf_op jit(solution)/shard_map/ppermute | solution.py:162
  80.8 20.5 %collective-permute-start.26 = (bf16[128,1024]{1,0:T(8,128)(2,1)}, bf16[128,1024]{1,0:T(8,128)(2,1)S(1)}, u32[]{:S(2)}, u32[]{:S(2)}) collective-permute-start(bf16[128,1024]{1,0:T(8,128)(2,1)} %get-tuple-element.103), channel_id=1, source_target_pairs={{0,2},{1,3},{2,0},{3,1},{4,6},{5,7},{6,4},{7,5},{8,10},{9,11},{10,... | collective-permute-start | bytes 786440 | tf_op jit(solution)/shard_map/ppermute | solution.py:162
  82.3 21.3 %collective-permute-start.35 = (bf16[128,1024]{1,0:T(8,128)(2,1)}, bf16[128,1024]{1,0:T(8,128)(2,1)S(1)}, u32[]{:S(2)}, u32[]{:S(2)}) collective-permute-start(bf16[128,1024]{1,0:T(8,128)(2,1)} %get-tuple-element.119), channel_id=1, source_target_pairs={{0,3},{1,2},{2,1},{3,0},{4,7},{5,6},{6,5},{7,4},{8,11},{9,10},{10,... | collective-permute-start | bytes 786440 | tf_op jit(solution)/shard_map/ppermute | solution.py:162
  83.7 21.4 %collective-permute-start.24 = (bf16[128,1024]{1,0:T(8,128)(2,1)}, bf16[128,1024]{1,0:T(8,128)(2,1)S(1)}, u32[]{:S(2)}, u32[]{:S(2)}) collective-permute-start(bf16[128,1024]{1,0:T(8,128)(2,1)} %get-tuple-element.99), channel_id=1, source_target_pairs={{0,6},{1,7},{2,4},{3,5},{4,2},{5,3},{6,0},{7,1},{8,14},{9,15},{10,... | collective-permute-start | bytes 786440 | tf_op jit(solution)/shard_map/ppermute | solution.py:162
  89.2 17.7 %collective-permute-start.31 = (bf16[128,1024]{1,0:T(8,128)(2,1)}, bf16[128,1024]{1,0:T(8,128)(2,1)S(1)}, u32[]{:S(2)}, u32[]{:S(2)}) collective-permute-start(bf16[128,1024]{1,0:T(8,128)(2,1)} %get-tuple-element.112), channel_id=1, source_target_pairs={{0,7},{1,6},{2,5},{3,4},{4,3},{5,2},{6,1},{7,0},{8,15},{9,14},{10,... | collective-permute-start | bytes 786440 | tf_op jit(solution)/shard_map/ppermute | solution.py:162
  101.3 13.9 %collective-permute-start.38 = (bf16[128,1024]{1,0:T(8,128)(2,1)S(1)}, bf16[128,1024]{1,0:T(8,128)(2,1)S(1)}, u32[]{:S(2)}, u32[]{:S(2)}) collective-permute-start(bf16[128,1024]{1,0:T(8,128)(2,1)S(1)} %copy-done.35), channel_id=1, source_target_pairs={{0,1},{1,0},{2,3},{3,2},{4,5},{5,4},{6,7},{7,6},{8,9},{9,8},{10,11... | collective-permute-start | bytes 786440 | tf_op jit(solution)/shard_map/ppermute | solution.py:161
  103.6 18.1 %collective-permute-start.36 = (bf16[128,1024]{1,0:T(8,128)(2,1)}, bf16[128,1024]{1,0:T(8,128)(2,1)S(1)}, u32[]{:S(2)}, u32[]{:S(2)}) collective-permute-start(bf16[128,1024]{1,0:T(8,128)(2,1)} %get-tuple-element.120), channel_id=1, source_target_pairs={{0,2},{1,3},{2,0},{3,1},{4,6},{5,7},{6,4},{7,5},{8,10},{9,11},{10,... | collective-permute-start | bytes 786440 | tf_op jit(solution)/shard_map/ppermute | solution.py:162
  106.9 15.4 %collective-permute-start.32 = (bf16[128,1024]{1,0:T(8,128)(2,1)}, bf16[128,1024]{1,0:T(8,128)(2,1)S(1)}, u32[]{:S(2)}, u32[]{:S(2)}) collective-permute-start(bf16[128,1024]{1,0:T(8,128)(2,1)} %get-tuple-element.113), channel_id=1, source_target_pairs={{0,4},{1,5},{2,6},{3,7},{4,0},{5,1},{6,2},{7,3},{8,12},{9,13},{10,... | collective-permute-start | bytes 786440 | tf_op jit(solution)/shard_map/ppermute | solution.py:162
  115.2 18.4 %collective-permute-start.34 = (bf16[128,1024]{1,0:T(8,128)(2,1)}, bf16[128,1024]{1,0:T(8,128)(2,1)S(1)}, u32[]{:S(2)}, u32[]{:S(2)}) collective-permute-start(bf16[128,1024]{1,0:T(8,128)(2,1)} %get-tuple-element.115), channel_id=1, source_target_pairs={{0,1},{1,0},{2,3},{3,2},{4,5},{5,4},{6,7},{7,6},{8,9},{9,8},{10,11... | collective-permute-start | bytes 786440 | tf_op jit(solution)/shard_map/ppermute | solution.py:161
  120.6 13.1 %collective-permute-start.29 = (bf16[128,1024]{1,0:T(8,128)(2,1)S(1)}, bf16[128,1024]{1,0:T(8,128)(2,1)S(1)}, u32[]{:S(2)}, u32[]{:S(2)}) collective-permute-start(bf16[128,1024]{1,0:T(8,128)(2,1)S(1)} %copy-done.34), channel_id=1, source_target_pairs={{0,5},{1,4},{2,7},{3,6},{4,1},{5,0},{6,3},{7,2},{8,13},{9,12},{10,... | collective-permute-start | bytes 786440 | tf_op jit(solution)/shard_map/ppermute | solution.py:162
  122.2 13.7 %collective-permute-start.33 = (bf16[128,1024]{1,0:T(8,128)(2,1)S(1)}, bf16[128,1024]{1,0:T(8,128)(2,1)S(1)}, u32[]{:S(2)}, u32[]{:S(2)}) collective-permute-start(bf16[128,1024]{1,0:T(8,128)(2,1)S(1)} %copy-done.33), channel_id=1, source_target_pairs={{0,7},{1,6},{2,5},{3,4},{4,3},{5,2},{6,1},{7,0},{8,15},{9,14},{10,... | collective-permute-start | bytes 786440 | tf_op jit(solution)/shard_map/ppermute | solution.py:162
  (54 other events, 562.6 us)

commit v3 on v2

--- a/solution.py
+++ b/solution.py
@@ -9,11 +9,12 @@
 
 RIM_BLOCKS = 2
 CHUNKS = 2
-STEP_PATCHES = 4
+STEP_PATCHES = 8
 PAD_ROWS = 16
 VMEM_BYTES = 60 * 1024 * 1024
 IN_FLIGHT = 4
 FIRST = 4
+ASSEMBLE_BYTES = 8 * 1024 * 1024
 EARLY = 3
 ASSEMBLE_BEFORE = 4
 
@@ -300,7 +301,7 @@
             ),
             out_shape=jax.ShapeDtypeStruct(prior_ensemble.shape, prior_ensemble.dtype),
             input_output_aliases={1 + len(pieces): 0} if base else {},
-            compiler_params=pltpu.CompilerParams(vmem_limit_bytes=VMEM_BYTES),
+            compiler_params=pltpu.CompilerParams(vmem_limit_bytes=ASSEMBLE_BYTES if base else VMEM_BYTES),
         )(place, *pieces, *base)
 
     analysis = None

time: 140 us -> 138 us (0.986)
  Pallas kernels: 39.8 us -> 36 us
  waiting for transfers between devices: 45 us -> 48.3 us
    ppermute x29, waiting for transfers between devices: 39.5 us -> 42.8 us  [partner(): sent.append(lax.ppermute(after_sent(x), 'mem', pairs))]
    pallas_call x3, Pallas kernels: 9.23 us -> 6.62 us  [assemble(): pl.pallas_call(functools.partial(assemble_kernel, moves, span), grid_spec...]
    unnamed x82 -> x72, local copies, waits for them, and re-layouts: 4.99 us -> 3.59 us
  transfers between devices with their start and end apart: 40 -> 40, of which waited for: 15 -> 15; matrix products, arithmetic and copies ran while one was open for 9% -> 9% of each run, Pallas kernels for 27% -> 25%
where the time goes in v3:
time: 138 us; the launch traced here: 137 us
  waiting for transfers between devices  48.3 us (35%)
  Pallas kernels  36 us (26%)
  starting transfers between devices  34.9 us (25%)
  local copies, waits for them, and re-layouts  12.8 us (9%)
  other arithmetic  3.82 us (3%)
    ppermute x29, waiting for transfers between devices, partner(): sent.append(lax.ppermute(after_sent(x), 'mem', pairs))  42.8 us
    ppermute x29, starting transfers between devices, partner(): sent.append(lax.ppermute(after_sent(x), 'mem', pairs))  28.4 us
    pallas_call x2, Pallas kernels, analyse(): pl.pallas_call(functools.partial(analyse_kernel, count, rows, span, obs_l...  17.5 us
    dynamic_slice x5, local copies, waits for them, and re-layouts, outgoing(): return lax.dynamic_slice_in_dim(source, first, chunk_span, 1)  9.1 us
    pallas_call x3, Pallas kernels, assemble(): pl.pallas_call(functools.partial(assemble_kernel, moves, span), grid_spec...  6.62 us
    pallas_call x1, Pallas kernels, per_device(): pl.pallas_call(functools.partial(prepare_kernel, count, rows, width, cent...  4.98 us
    ppermute x1, waiting for transfers between devices, per_device(): after = lax.ppermute(both[:, :, :rim], 'band', down)  4.74 us
    unnamed x72, local copies, waits for them, and re-layouts  3.59 us
  transfers between devices with their start and end apart: 40, of which 15 were waited for; matrix products, arithmetic and copies ran while one was open for 9% of the time, Pallas kernels for 25%

profile of v3, /device:TPU:0, one launch (start us, length us, event | category | flops | bytes accessed | tf_op | source)
XLA Modules:
  0.0 136.9 jit_solution(6732408565484679892)
XLA Ops:
  1.6 3.0 %collective-permute-start.4 = (bf16[128,1024]{1,0:T(8,128)(2,1)S(1)}, bf16[128,1024]{1,0:T(8,128)(2,1)S(1)}, u32[]{:S(2)}, u32[]{:S(2)}) collective-permute-start(bf16[128,1024]{1,0:T(8,128)(2,1)S(1)} %constant_dynamic-slice_fusion.17), channel_id=1, source_target_pairs={{0,2},{1,3},{2,0},{3,1},{4,6},{5,7},{6,4},{7,5},{8,10},{9,11},{10,... | collective-permute-start | bytes 786440 | tf_op jit(solution)/shard_map/ppermute | solution.py:163
  6.3 1.7 %constant_dynamic-slice_fusion.15 = bf16[128,1024]{1,0:T(8,128)(2,1)} fusion(bf16[128,16384]{1,0:T(8,128)(2,1)} %refs_0_.3, s32[]{:T(128)S(6)} %select_n.56), kind=kLoop, calls=%fused_computation.27 | loop fusion | bytes 524292 | tf_op jit(solution)/shard_map/dynamic_slice | solution.py:191
  9.7 2.1 %collective-permute-start.11 = (bf16[128,1024]{1,0:T(8,128)(2,1)}, bf16[128,1024]{1,0:T(8,128)(2,1)S(1)}, u32[]{:S(2)}, u32[]{:S(2)}) collective-permute-start(bf16[128,1024]{1,0:T(8,128)(2,1)} %constant_dynamic-slice_fusion.15), channel_id=1, source_target_pairs={{0,6},{1,7},{2,4},{3,5},{4,2},{5,3},{6,0},{7,1},{8,14},{9,15},{10,... | collective-permute-start | bytes 786440 | tf_op jit(solution)/shard_map/ppermute | solution.py:163
  13.4 3.5 %collective-permute-start.5 = (bf16[2,128,256]{2,1,0:T(8,128)(2,1)S(1)}, bf16[2,128,256]{2,1,0:T(8,128)(2,1)S(1)}, u32[]{:S(2)}, u32[]{:S(2)}) collective-permute-start(bf16[2,128,256]{2,1,0:T(8,128)(2,1)S(1)} %get-tuple-element.145), channel_id=1, source_target_pairs={{0,8},{8,16},{16,24},{1,9},{9,17},{17,25},{2,10},{10,18},{18,26},{... | collective-permute-start | bytes 393224 | tf_op jit(solution)/shard_map/ppermute | solution.py:204
  16.9 3.1 %constant_dynamic-slice_fusion = (bf16[128,1024]{1,0:T(8,128)(2,1)}, bf16[128,1024]{1,0:T(8,128)(2,1)}, bf16[128,1024]{1,0:T(8,128)(2,1)}, bf16[128,1024]{1,0:T(...) fusion(bf16[128,16384]{1,0:T(8,128)(2,1)} %refs_0_.3, ...), kind=kLoop, calls=%fused_computation.12 | loop fusion | bytes 5242920 | tf_op jit(solution)/shard_map/dynamic_slice | solution.py:191
  22.7 4.7 %collective-permute-done.6 = bf16[2,128,256]{2,1,0:T(8,128)(2,1)S(1)} collective-permute-done((bf16[2,128,256]{2,1,0:T(8,128)(2,1)S(1)}, bf16[2,128,256]{2,1,0:T(8,128)(2,1)S(1)}, u32[]{:S(2)}, u32[]{:S(2)}) %collective-permute-start.6) | collective-permute-done | bytes 131104 | tf_op jit(solution)/shard_map/ppermute | solution.py:205
  29.7 2.1 %collective-permute-done.8.refs_5_ = bf16[128,1024]{1,0:T(8,128)(2,1)S(1)} collective-permute-done((bf16[128,1024]{1,0:T(8,128)(2,1)S(1)}, bf16[128,1024]{1,0:T(8,128)(2,1)S(1)}, u32[]{:S(2)}, u32[]{:S(2)}) %collective-permute-start.8) | collective-permute-done | bytes 262176 | tf_op jit(solution)/shard_map/ppermute | solution.py:163
  32.9 2.1 %shard_map.87.refs_11_ = f32[8,128,128]{2,1,0:T(8,128)} custom-call(f32[8,128,128]{2,1,0:T(8,128)} %loc_ref.1), custom_call_target="tpu_custom_call" | custom-call | tf_op jit(solution)/shard_map/pallas_call | solution.py:181
  35.6 3.3 %shard_map.86.select_ref = f32[32,128]{1,0:T(8,128)} custom-call(s32[128]{0:T(128)} %owner_ref.1, s32[2]{0:T(128)} %pad_add_fusion.place_ref), custom_call_target="tpu_custom_call" | custom-call | tf_op jit(solution)/shard_map/pallas_call | solution.py:171
  39.8 3.8 %collective-permute-done.2.refs_7_ = bf16[128,1024]{1,0:T(8,128)(2,1)} collective-permute-done((bf16[128,1024]{1,0:T(8,128)(2,1)}, bf16[128,1024]{1,0:T(8,128)(2,1)}, u32[]{:S(2)}, u32[]{:S(2)}) %collective-permute-start.2) | collective-permute-done | bytes 262176 | tf_op jit(solution)/shard_map/ppermute | solution.py:163
  45.1 9.3 %collective-permute-done.17.refs_4_ = bf16[2,128,768]{2,1,0:T(8,128)(2,1)S(1)} collective-permute-done((bf16[2,128,768]{2,1,0:T(8,128)(2,1)S(1)}, bf16[2,128,768]{2,1,0:T(8,128)(2,1)S(1)}, u32[]{:S(2)}, u32[]{:S(2)}) %collective-permute-start.17) | collective-permute-done | bytes 393248 | tf_op jit(solution)/shard_map/ppermute | solution.py:163
  55.5 2.3 %collective-permute-done.3.refs_2_ = bf16[128,1024]{1,0:T(8,128)(2,1)S(1)} collective-permute-done((bf16[128,1024]{1,0:T(8,128)(2,1)}, bf16[128,1024]{1,0:T(8,128)(2,1)S(1)}, u32[]{:S(2)}, u32[]{:S(2)}) %collective-permute-start.3) | collective-permute-done | bytes 262176 | tf_op jit(solution)/shard_map/ppermute | solution.py:163
  58.2 2.7 %collective-permute-start.18 = (bf16[128,1024]{1,0:T(8,128)(2,1)}, bf16[128,1024]{1,0:T(8,128)(2,1)}, u32[]{:S(2)}, u32[]{:S(2)}) collective-permute-start(bf16[128,1024]{1,0:T(8,128)(2,1)} %get-tuple-element.87), channel_id=1, source_target_pairs={{0,6},{1,7},{2,4},{3,5},{4,2},{5,3},{6,0},{7,1},{8,14},{9,15},{10,... | collective-permute-start | bytes 786440 | tf_op jit(solution)/shard_map/ppermute | solution.py:163
  60.9 2.9 %collective-permute-done.13.refs_4_ = bf16[128,1024]{1,0:T(8,128)(2,1)S(1)} collective-permute-done((bf16[128,1024]{1,0:T(8,128)(2,1)}, bf16[128,1024]{1,0:T(8,128)(2,1)S(1)}, u32[]{:S(2)}, u32[]{:S(2)}) %collective-permute-start.13) | collective-permute-done | bytes 262176 | tf_op jit(solution)/shard_map/ppermute | solution.py:163
  65.6 5.0 %shard_map.88 = (bf16[656,1024]{1,0:T(8,128)(2,1)}, bf16[1024,640]{1,0:T(8,128)(2,1)}, f32[640,128]{1,0:T(8,128)}) custom-call(s32[2]{0:T(128)} %pad_add_fusion.place_ref, bf16[2,128,768]{2,1,0:T(8,128)(2,1)} %copy-done.2, bf16[2,128,768]{2,1,0:T(8,128)(2,1)} %copy-done.6, bf16[2,128,768]{2,1,0:T(8,128)(2,1)} %copy-done.3, bf16[2,128,768]{2,1,0:T(8,128)(2,1)} %copy-done.7, ...), custom_call_target="tpu_custom_call" | custom-call | tf_op jit(solution)/shard_map/pallas_call | solution.py:230
  70.6 8.8 %shard_map.90 = (bf16[128,1024]{1,0:T(8,128)(2,1)}, bf16[128,1024]{1,0:T(8,128)(2,1)}, bf16[128,1024]{1,0:T(8,128)(2,1)}, bf16[128,1024]{1,0:T(8,128)(2,1)}, bf1...) custom-call(s32[2]{0:T(128)} %pad_add_fusion.place_ref, ...), custom_call_target="tpu_custom_call" | custom-call | tf_op jit(solution)/shard_map/pallas_call | solution.py:260
  81.9 2.0 %collective-permute-done.15.refs_5_ = bf16[128,1024]{1,0:T(8,128)(2,1)} collective-permute-done((bf16[128,1024]{1,0:T(8,128)(2,1)}, bf16[128,1024]{1,0:T(8,128)(2,1)}, u32[]{:S(2)}, u32[]{:S(2)}) %collective-permute-start.15) | collective-permute-done | bytes 262176 | tf_op jit(solution)/shard_map/ppermute | solution.py:163
  84.3 4.7 %collective-permute-done.30.refs_2_ = bf16[128,1024]{1,0:T(8,128)(2,1)S(1)} collective-permute-done((bf16[128,1024]{1,0:T(8,128)(2,1)}, bf16[128,1024]{1,0:T(8,128)(2,1)S(1)}, u32[]{:S(2)}, u32[]{:S(2)}) %collective-permute-start.30) | collective-permute-done | bytes 262176 | tf_op jit(solution)/shard_map/ppermute | solution.py:163
  90.1 8.6 %shard_map.89 = (bf16[128,1024]{1,0:T(8,128)(2,1)}, bf16[128,1024]{1,0:T(8,128)(2,1)}, bf16[128,1024]{1,0:T(8,128)(2,1)}, bf16[128,1024]{1,0:T(8,128)(2,1)}, bf1...) custom-call(s32[2]{0:T(128)} %pad_add_fusion.place_ref, ...), custom_call_target="tpu_custom_call" | custom-call | tf_op jit(solution)/shard_map/pallas_call | solution.py:260
  107.0 5.0 %collective-permute-done.25 = f32[32,128]{1,0:T(8,128)S(1)} collective-permute-done((f32[32,128]{1,0:T(8,128)S(1)}, f32[32,128]{1,0:T(8,128)S(1)}, u32[]{:S(2)}, u32[]{:S(2)}) %collective-permute-start.25) | collective-permute-done | bytes 16416 | tf_op jit(solution)/shard_map/ppermute | solution.py:163
  114.7 1.7 %collective-permute-start.37 = (bf16[128,1024]{1,0:T(8,128)(2,1)}, bf16[128,1024]{1,0:T(8,128)(2,1)S(1)}, u32[]{:S(2)}, u32[]{:S(2)}) collective-permute-start(bf16[128,1024]{1,0:T(8,128)(2,1)} %get-tuple-element.122), channel_id=1, source_target_pairs={{0,6},{1,7},{2,4},{3,5},{4,2},{5,3},{6,0},{7,1},{8,14},{9,15},{10,... | collective-permute-start | bytes 786440 | tf_op jit(solution)/shard_map/ppermute | solution.py:163
  116.4 3.5 %shard_map.91.refs_5_ = bf16[128,16384]{1,0:T(8,128)(2,1)} custom-call(s32[2]{0:T(128)} %pad_add_fusion.place_ref, bf16[128,1024]{1,0:T(8,128)(2,1)} %get-tuple-element.124.refs_0_, bf16[128,1024]{1,0:T(8,128)(2,1)} %copy-done.19, bf16[128,1024]{1,0:T(8,128)(2,1)} %copy-done.17, bf16[128,1024]{1,0:T(8,128)(2,1)} %copy-done.21, bf16[128,1024]{1,0:T(8,128)(2,1)} %copy-done.20, ...), custom_call_target="tpu_custom_call" | custom-call | tf_op jit(solution)/shard_map/pallas_call | solution.py:292
  125.3 4.0 %collective-permute-done.39.refs_4_ = bf16[128,1024]{1,0:T(8,128)(2,1)S(1)} collective-permute-done((bf16[128,1024]{1,0:T(8,128)(2,1)S(1)}, bf16[128,1024]{1,0:T(8,128)(2,1)S(1)}, u32[]{:S(2)}, u32[]{:S(2)}) %collective-permute-start.39) | collective-permute-done | bytes 262176 | tf_op jit(solution)/shard_map/ppermute | solution.py:163
  131.0 4.5 %collective-permute-done.33.refs_1_ = bf16[128,1024]{1,0:T(8,128)(2,1)S(1)} collective-permute-done((bf16[128,1024]{1,0:T(8,128)(2,1)S(1)}, bf16[128,1024]{1,0:T(8,128)(2,1)S(1)}, u32[]{:S(2)}, u32[]{:S(2)}) %collective-permute-start.33) | collective-permute-done | bytes 262176 | tf_op jit(solution)/shard_map/ppermute | solution.py:163
  (151 shorter events, 41.4 us)
Async XLA Ops:
  9.6 18.6 %collective-permute-start.16 = (bf16[128,1024]{1,0:T(8,128)(2,1)}, bf16[128,1024]{1,0:T(8,128)(2,1)S(1)}, u32[]{:S(2)}, u32[]{:S(2)}) collective-permute-start(bf16[128,1024]{1,0:T(8,128)(2,1)} %constant_dynamic-slice_fusion.14), channel_id=1, source_target_pairs={{0,3},{1,2},{2,1},{3,0},{4,7},{5,6},{6,5},{7,4},{8,11},{9,10},{10,... | collective-permute-start | bytes 786440 | tf_op jit(solution)/shard_map/ppermute | solution.py:163
  9.7 18.0 %collective-permute-start.11 = (bf16[128,1024]{1,0:T(8,128)(2,1)}, bf16[128,1024]{1,0:T(8,128)(2,1)S(1)}, u32[]{:S(2)}, u32[]{:S(2)}) collective-permute-start(bf16[128,1024]{1,0:T(8,128)(2,1)} %constant_dynamic-slice_fusion.15), channel_id=1, source_target_pairs={{0,6},{1,7},{2,4},{3,5},{4,2},{5,3},{6,0},{7,1},{8,14},{9,15},{10,... | collective-permute-start | bytes 786440 | tf_op jit(solution)/shard_map/ppermute | solution.py:163
  11.8 17.9 %collective-permute-start.1 = (bf16[128,1024]{1,0:T(8,128)(2,1)}, bf16[128,1024]{1,0:T(8,128)(2,1)S(1)}, u32[]{:S(2)}, u32[]{:S(2)}) collective-permute-start(bf16[128,1024]{1,0:T(8,128)(2,1)} %constant_dynamic-slice_fusion.16), channel_id=1, source_target_pairs={{0,4},{1,5},{2,6},{3,7},{4,0},{5,1},{6,2},{7,3},{8,12},{9,13},{10,... | collective-permute-start | bytes 786440 | tf_op jit(solution)/shard_map/ppermute | solution.py:163
  27.6 12.1 %collective-permute-start.12 = (bf16[2,128,768]{2,1,0:T(8,128)(2,1)S(1)}, bf16[2,128,768]{2,1,0:T(8,128)(2,1)S(1)}, u32[]{:S(2)}, u32[]{:S(2)}) collective-permute-start(bf16[2,128,768]{2,1,0:T(8,128)(2,1)S(1)} %get-tuple-element.81), channel_id=1, source_target_pairs={{0,2},{1,3},{2,0},{3,1},{4,6},{5,7},{6,4},{7,5},{8,10},{9,11},{10,... | collective-permute-start | bytes 1179656 | tf_op jit(solution)/shard_map/ppermute | solution.py:163
  28.2 26.2 %collective-permute-start.17 = (bf16[2,128,768]{2,1,0:T(8,128)(2,1)S(1)}, bf16[2,128,768]{2,1,0:T(8,128)(2,1)S(1)}, u32[]{:S(2)}, u32[]{:S(2)}) collective-permute-start(bf16[2,128,768]{2,1,0:T(8,128)(2,1)S(1)} %get-tuple-element.86), channel_id=1, source_target_pairs={{0,4},{1,5},{2,6},{3,7},{4,0},{5,1},{6,2},{7,3},{8,12},{9,13},{10,... | collective-permute-start | bytes 1179656 | tf_op jit(solution)/shard_map/ppermute | solution.py:163
  29.7 13.8 %collective-permute-start.2 = (bf16[128,1024]{1,0:T(8,128)(2,1)}, bf16[128,1024]{1,0:T(8,128)(2,1)}, u32[]{:S(2)}, u32[]{:S(2)}) collective-permute-start(bf16[128,1024]{1,0:T(8,128)(2,1)} %get-tuple-element.71), channel_id=1, source_target_pairs={{0,7},{1,6},{2,5},{3,4},{4,3},{5,2},{6,1},{7,0},{8,15},{9,14},{10,... | collective-permute-start | bytes 786440 | tf_op jit(solution)/shard_map/ppermute | solution.py:163
  32.6 22.2 %collective-permute-start.9 = (bf16[2,128,768]{2,1,0:T(8,128)(2,1)S(1)}, bf16[2,128,768]{2,1,0:T(8,128)(2,1)S(1)}, u32[]{:S(2)}, u32[]{:S(2)}) collective-permute-start(bf16[2,128,768]{2,1,0:T(8,128)(2,1)S(1)} %get-tuple-element.78), channel_id=1, source_target_pairs={{0,6},{1,7},{2,4},{3,5},{4,2},{5,3},{6,0},{7,1},{8,14},{9,15},{10,... | collective-permute-start | bytes 1179656 | tf_op jit(solution)/shard_map/ppermute | solution.py:163
  38.8 16.1 %collective-permute-start.7 = (bf16[2,128,768]{2,1,0:T(8,128)(2,1)S(1)}, bf16[2,128,768]{2,1,0:T(8,128)(2,1)S(1)}, u32[]{:S(2)}, u32[]{:S(2)}) collective-permute-start(bf16[2,128,768]{2,1,0:T(8,128)(2,1)S(1)} %get-tuple-element.75.refs_0_), channel_id=1, source_target_pairs={{0,1},{1,0},{2,3},{3,2},{4,5},{5,4},{6,7},{7,6},{8,9},{9,8},{10,11... | collective-permute-start | bytes 1179656 | tf_op jit(solution)/shard_map/ppermute | solution.py:162
  39.8 18.0 %collective-permute-start.14 = (bf16[2,128,768]{2,1,0:T(8,128)(2,1)S(1)}, bf16[2,128,768]{2,1,0:T(8,128)(2,1)S(1)}, u32[]{:S(2)}, u32[]{:S(2)}) collective-permute-start(bf16[2,128,768]{2,1,0:T(8,128)(2,1)S(1)} %collective-permute-done.12.refs_2_), channel_id=1, source_target_pairs={{0,1},{1,0},{2,3},{3,2},{4,5},{5,4},{6,7},{7,6},{8,9},{9,8},{10,11... | collective-permute-start | bytes 1179656 | tf_op jit(solution)/shard_map/ppermute | solution.py:162
  43.5 14.2 %collective-permute-start.3 = (bf16[128,1024]{1,0:T(8,128)(2,1)}, bf16[128,1024]{1,0:T(8,128)(2,1)S(1)}, u32[]{:S(2)}, u32[]{:S(2)}) collective-permute-start(bf16[128,1024]{1,0:T(8,128)(2,1)} %get-tuple-element.72), channel_id=1, source_target_pairs={{0,2},{1,3},{2,0},{3,1},{4,6},{5,7},{6,4},{7,5},{8,10},{9,11},{10,... | collective-permute-start | bytes 786440 | tf_op jit(solution)/shard_map/ppermute | solution.py:163
  57.7 12.8 %collective-permute-start.22 = (bf16[128,1024]{1,0:T(8,128)(2,1)}, bf16[128,1024]{1,0:T(8,128)(2,1)}, u32[]{:S(2)}, u32[]{:S(2)}) collective-permute-start(bf16[128,1024]{1,0:T(8,128)(2,1)} %get-tuple-element.130), channel_id=1, source_target_pairs={{0,1},{1,0},{2,3},{3,2},{4,5},{5,4},{6,7},{7,6},{8,9},{9,8},{10,11... | collective-permute-start | bytes 786440 | tf_op jit(solution)/shard_map/ppermute | solution.py:162
  57.8 21.7 %collective-permute-start.10 = (bf16[128,1024]{1,0:T(8,128)(2,1)}, bf16[128,1024]{1,0:T(8,128)(2,1)}, u32[]{:S(2)}, u32[]{:S(2)}) collective-permute-start(bf16[128,1024]{1,0:T(8,128)(2,1)} %get-tuple-element.79), channel_id=1, source_target_pairs={{0,3},{1,2},{2,1},{3,0},{4,7},{5,6},{6,5},{7,4},{8,11},{9,10},{10,... | collective-permute-start | bytes 786440 | tf_op jit(solution)/shard_map/ppermute | solution.py:163
  58.2 22.1 %collective-permute-start.18 = (bf16[128,1024]{1,0:T(8,128)(2,1)}, bf16[128,1024]{1,0:T(8,128)(2,1)}, u32[]{:S(2)}, u32[]{:S(2)}) collective-permute-start(bf16[128,1024]{1,0:T(8,128)(2,1)} %get-tuple-element.87), channel_id=1, source_target_pairs={{0,6},{1,7},{2,4},{3,5},{4,2},{5,3},{6,0},{7,1},{8,14},{9,15},{10,... | collective-permute-start | bytes 786440 | tf_op jit(solution)/shard_map/ppermute | solution.py:163
  63.7 20.2 %collective-permute-start.15 = (bf16[128,1024]{1,0:T(8,128)(2,1)}, bf16[128,1024]{1,0:T(8,128)(2,1)}, u32[]{:S(2)}, u32[]{:S(2)}) collective-permute-start(bf16[128,1024]{1,0:T(8,128)(2,1)} %get-tuple-element.84), channel_id=1, source_target_pairs={{0,5},{1,4},{2,7},{3,6},{4,1},{5,0},{6,3},{7,2},{8,13},{9,12},{10,... | collective-permute-start | bytes 786440 | tf_op jit(solution)/shard_map/ppermute | solution.py:163
  64.4 17.3 %collective-permute-start.20 = (bf16[128,1024]{1,0:T(8,128)(2,1)}, bf16[128,1024]{1,0:T(8,128)(2,1)}, u32[]{:S(2)}, u32[]{:S(2)}) collective-permute-start(bf16[128,1024]{1,0:T(8,128)(2,1)} %get-tuple-element.89), channel_id=1, source_target_pairs={{0,7},{1,6},{2,5},{3,4},{4,3},{5,2},{6,1},{7,0},{8,15},{9,14},{10,... | collective-permute-start | bytes 786440 | tf_op jit(solution)/shard_map/ppermute | solution.py:163
  80.3 20.0 %collective-permute-start.26 = (bf16[128,1024]{1,0:T(8,128)(2,1)}, bf16[128,1024]{1,0:T(8,128)(2,1)S(1)}, u32[]{:S(2)}, u32[]{:S(2)}) collective-permute-start(bf16[128,1024]{1,0:T(8,128)(2,1)} %get-tuple-element.103), channel_id=1, source_target_pairs={{0,2},{1,3},{2,0},{3,1},{4,6},{5,7},{6,4},{7,5},{8,10},{9,11},{10,... | collective-permute-start | bytes 786440 | tf_op jit(solution)/shard_map/ppermute | solution.py:163
  81.8 21.3 %collective-permute-start.35 = (bf16[128,1024]{1,0:T(8,128)(2,1)}, bf16[128,1024]{1,0:T(8,128)(2,1)S(1)}, u32[]{:S(2)}, u32[]{:S(2)}) collective-permute-start(bf16[128,1024]{1,0:T(8,128)(2,1)} %get-tuple-element.119), channel_id=1, source_target_pairs={{0,3},{1,2},{2,1},{3,0},{4,7},{5,6},{6,5},{7,4},{8,11},{9,10},{10,... | collective-permute-start | bytes 786440 | tf_op jit(solution)/shard_map/ppermute | solution.py:163
  83.9 20.6 %collective-permute-start.24 = (bf16[128,1024]{1,0:T(8,128)(2,1)}, bf16[128,1024]{1,0:T(8,128)(2,1)S(1)}, u32[]{:S(2)}, u32[]{:S(2)}) collective-permute-start(bf16[128,1024]{1,0:T(8,128)(2,1)} %get-tuple-element.99), channel_id=1, source_target_pairs={{0,6},{1,7},{2,4},{3,5},{4,2},{5,3},{6,0},{7,1},{8,14},{9,15},{10,... | collective-permute-start | bytes 786440 | tf_op jit(solution)/shard_map/ppermute | solution.py:163
  89.1 17.3 %collective-permute-start.31 = (bf16[128,1024]{1,0:T(8,128)(2,1)}, bf16[128,1024]{1,0:T(8,128)(2,1)S(1)}, u32[]{:S(2)}, u32[]{:S(2)}) collective-permute-start(bf16[128,1024]{1,0:T(8,128)(2,1)} %get-tuple-element.112), channel_id=1, source_target_pairs={{0,7},{1,6},{2,5},{3,4},{4,3},{5,2},{6,1},{7,0},{8,15},{9,14},{10,... | collective-permute-start | bytes 786440 | tf_op jit(solution)/shard_map/ppermute | solution.py:163
  100.3 14.4 %collective-permute-start.38 = (bf16[128,1024]{1,0:T(8,128)(2,1)S(1)}, bf16[128,1024]{1,0:T(8,128)(2,1)S(1)}, u32[]{:S(2)}, u32[]{:S(2)}) collective-permute-start(bf16[128,1024]{1,0:T(8,128)(2,1)S(1)} %copy-done.30), channel_id=1, source_target_pairs={{0,1},{1,0},{2,3},{3,2},{4,5},{5,4},{6,7},{7,6},{8,9},{9,8},{10,11... | collective-permute-start | bytes 786440 | tf_op jit(solution)/shard_map/ppermute | solution.py:162
  103.1 18.1 %collective-permute-start.36 = (bf16[128,1024]{1,0:T(8,128)(2,1)}, bf16[128,1024]{1,0:T(8,128)(2,1)S(1)}, u32[]{:S(2)}, u32[]{:S(2)}) collective-permute-start(bf16[128,1024]{1,0:T(8,128)(2,1)} %get-tuple-element.120), channel_id=1, source_target_pairs={{0,2},{1,3},{2,0},{3,1},{4,6},{5,7},{6,4},{7,5},{8,10},{9,11},{10,... | collective-permute-start | bytes 786440 | tf_op jit(solution)/shard_map/ppermute | solution.py:163
  106.4 15.3 %collective-permute-start.32 = (bf16[128,1024]{1,0:T(8,128)(2,1)}, bf16[128,1024]{1,0:T(8,128)(2,1)S(1)}, u32[]{:S(2)}, u32[]{:S(2)}) collective-permute-start(bf16[128,1024]{1,0:T(8,128)(2,1)} %get-tuple-element.113), channel_id=1, source_target_pairs={{0,4},{1,5},{2,6},{3,7},{4,0},{5,1},{6,2},{7,3},{8,12},{9,13},{10,... | collective-permute-start | bytes 786440 | tf_op jit(solution)/shard_map/ppermute | solution.py:163
  114.7 16.3 %collective-permute-start.34 = (bf16[128,1024]{1,0:T(8,128)(2,1)}, bf16[128,1024]{1,0:T(8,128)(2,1)S(1)}, u32[]{:S(2)}, u32[]{:S(2)}) collective-permute-start(bf16[128,1024]{1,0:T(8,128)(2,1)} %get-tuple-element.115), channel_id=1, source_target_pairs={{0,1},{1,0},{2,3},{3,2},{4,5},{5,4},{6,7},{7,6},{8,9},{9,8},{10,11... | collective-permute-start | bytes 786440 | tf_op jit(solution)/shard_map/ppermute | solution.py:162
  121.7 13.8 %collective-permute-start.33 = (bf16[128,1024]{1,0:T(8,128)(2,1)S(1)}, bf16[128,1024]{1,0:T(8,128)(2,1)S(1)}, u32[]{:S(2)}, u32[]{:S(2)}) collective-permute-start(bf16[128,1024]{1,0:T(8,128)(2,1)S(1)} %copy-done.28), channel_id=1, source_target_pairs={{0,7},{1,6},{2,5},{3,4},{4,3},{5,2},{6,1},{7,0},{8,15},{9,14},{10,... | collective-permute-start | bytes 786440 | tf_op jit(solution)/shard_map/ppermute | solution.py:163
  (49 other events, 595.5 us)

commit v4 on v3

--- a/solution.py
+++ b/solution.py
@@ -48,7 +48,7 @@
     for i, piece in enumerate(pieces):
         place = slice(i * rows, (i + 1) * rows)
         dev = piece[0, :, window].astype(jnp.float32) - centre
-        ydt_ref[:width, place] = jnp.transpose(dev).astype(jnp.bfloat16)
+        ydt_ref[:width, place] = jnp.transpose(dev.astype(jnp.bfloat16))
         solved_ref[place, :] = piece[1, :, window]
     ydt_ref[width:, :] = jnp.ones((ydt_ref.shape[0] - width, members), jnp.bfloat16)
     ysum_ref[...] = jnp.dot(
@@ -223,7 +223,7 @@
     for chunk in range(1, CHUNKS):
         for flip in order:
             if flip not in got[chunk]:
-                after = [pieces[flip - 2]] if chunk == 1 and flip & 1 and flip > 1 else []
+                after = [pieces[flip - 2]] if chunk == 1 and flip & 1 and 1 < flip < count - 1 else []
                 got[chunk][flip] = partner(outgoing(source, flip, chunk), flip, after)
     priors = [[pieces_of[i] for i in range(1, count)] for pieces_of in got]
 

time: 138 us -> 144 us (1.043)
  starting transfers between devices: 34.9 us -> 40.6 us
  waiting for transfers between devices: 48.3 us -> 50.4 us
    ppermute x29, starting transfers between devices: 28.4 us -> 33.9 us  [partner(): sent.append(lax.ppermute(after_sent(x), 'mem', pairs))]
    ppermute x29, waiting for transfers between devices: 42.8 us -> 44.9 us  [partner(): sent.append(lax.ppermute(after_sent(x), 'mem', pairs))]
    unnamed x72 -> x74, local copies, waits for them, and re-layouts: 3.59 us -> 2.88 us
  transfers between devices with their start and end apart: 40 -> 40, of which waited for: 15 -> 11; matrix products, arithmetic and copies ran while one was open for 9% -> 9% of each run, Pallas kernels for 25% -> 24%
where the time goes in v4:
time: 144 us; the launch traced here: 143 us
  waiting for transfers between devices  50.4 us (35%)
  starting transfers between devices  40.6 us (28%)
  Pallas kernels  35.9 us (25%)
  local copies, waits for them, and re-layouts  11.5 us (8%)
  other arithmetic  3.78 us (3%)
    ppermute x29, waiting for transfers between devices, partner(): sent.append(lax.ppermute(after_sent(x), 'mem', pairs))  44.9 us
    ppermute x29, starting transfers between devices, partner(): sent.append(lax.ppermute(after_sent(x), 'mem', pairs))  33.9 us
    pallas_call x2, Pallas kernels, analyse(): pl.pallas_call(functools.partial(analyse_kernel, count, rows, span, obs_l...  17.5 us
    dynamic_slice x5, local copies, waits for them, and re-layouts, outgoing(): return lax.dynamic_slice_in_dim(source, first, chunk_span, 1)  8.5 us
    pallas_call x3, Pallas kernels, assemble(): pl.pallas_call(functools.partial(assemble_kernel, moves, span), grid_spec...  6.62 us
    pallas_call x1, Pallas kernels, per_device(): pl.pallas_call(functools.partial(prepare_kernel, count, rows, width, cent...  4.93 us
    ppermute x1, waiting for transfers between devices, per_device(): after = lax.ppermute(both[:, :, :rim], 'band', down)  4.74 us
    ppermute x1, starting transfers between devices, per_device(): before = lax.ppermute(both[:, :, -rim:], 'band', up)  3.49 us
  transfers between devices with their start and end apart: 40, of which 11 were waited for; matrix products, arithmetic and copies ran while one was open for 9% of the time, Pallas kernels for 24%

profile of v4, /device:TPU:0, one launch (start us, length us, event | category | flops | bytes accessed | tf_op | source)
XLA Modules:
  0.0 143.2 jit_solution(16951834691407673593)
XLA Ops:
  1.6 3.0 %collective-permute-start.4 = (bf16[128,1024]{1,0:T(8,128)(2,1)S(1)}, bf16[128,1024]{1,0:T(8,128)(2,1)S(1)}, u32[]{:S(2)}, u32[]{:S(2)}) collective-permute-start(bf16[128,1024]{1,0:T(8,128)(2,1)S(1)} %constant_dynamic-slice_fusion.17), channel_id=1, source_target_pairs={{0,2},{1,3},{2,0},{3,1},{4,6},{5,7},{6,4},{7,5},{8,10},{9,11},{10,... | collective-permute-start | bytes 786440 | tf_op jit(solution)/shard_map/ppermute | solution.py:163
  4.6 1.7 %constant_dynamic-slice_fusion.16 = bf16[128,1024]{1,0:T(8,128)(2,1)} fusion(bf16[128,16384]{1,0:T(8,128)(2,1)} %refs_0_.3, s32[]{:T(128)S(6)} %select_n.55), kind=kLoop, calls=%fused_computation.28 | loop fusion | bytes 524292 | tf_op jit(solution)/shard_map/dynamic_slice | solution.py:191
  7.3 1.7 %constant_dynamic-slice_fusion.14 = bf16[128,1024]{1,0:T(8,128)(2,1)} fusion(bf16[128,16384]{1,0:T(8,128)(2,1)} %refs_0_.3, s32[]{:T(128)S(6)} %select_n.57), kind=kLoop, calls=%fused_computation.26 | loop fusion | bytes 524292 | tf_op jit(solution)/shard_map/dynamic_slice | solution.py:191
  9.0 2.1 %collective-permute-start.11 = (bf16[128,1024]{1,0:T(8,128)(2,1)S(1)}, bf16[128,1024]{1,0:T(8,128)(2,1)S(1)}, u32[]{:S(2)}, u32[]{:S(2)}) collective-permute-start(bf16[128,1024]{1,0:T(8,128)(2,1)S(1)} %constant_dynamic-slice_fusion.15), channel_id=1, source_target_pairs={{0,6},{1,7},{2,4},{3,5},{4,2},{5,3},{6,0},{7,1},{8,14},{9,15},{10,... | collective-permute-start | bytes 786440 | tf_op jit(solution)/shard_map/ppermute | solution.py:163
  12.7 3.5 %collective-permute-start.5 = (bf16[2,128,256]{2,1,0:T(8,128)(2,1)S(1)}, bf16[2,128,256]{2,1,0:T(8,128)(2,1)S(1)}, u32[]{:S(2)}, u32[]{:S(2)}) collective-permute-start(bf16[2,128,256]{2,1,0:T(8,128)(2,1)S(1)} %get-tuple-element.143), channel_id=1, source_target_pairs={{0,8},{8,16},{16,24},{1,9},{9,17},{17,25},{2,10},{10,18},{18,26},{... | collective-permute-start | bytes 393224 | tf_op jit(solution)/shard_map/ppermute | solution.py:204
  16.2 3.2 %constant_dynamic-slice_fusion = (bf16[128,1024]{1,0:T(8,128)(2,1)}, bf16[128,1024]{1,0:T(8,128)(2,1)}, bf16[128,1024]{1,0:T(8,128)(2,1)}, bf16[128,1024]{1,0:T(...) fusion(bf16[128,16384]{1,0:T(8,128)(2,1)} %refs_0_.3, ...), kind=kLoop, calls=%fused_computation.12 | loop fusion | bytes 5242920 | tf_op jit(solution)/shard_map/dynamic_slice | solution.py:191
  22.1 4.7 %collective-permute-done.6 = bf16[2,128,256]{2,1,0:T(8,128)(2,1)S(1)} collective-permute-done((bf16[2,128,256]{2,1,0:T(8,128)(2,1)S(1)}, bf16[2,128,256]{2,1,0:T(8,128)(2,1)S(1)}, u32[]{:S(2)}, u32[]{:S(2)}) %collective-permute-start.6) | collective-permute-done | bytes 131104 | tf_op jit(solution)/shard_map/ppermute | solution.py:205
  28.2 2.1 %shard_map.87.refs_11_ = f32[8,128,128]{2,1,0:T(8,128)} custom-call(f32[8,128,128]{2,1,0:T(8,128)} %loc_ref.1), custom_call_target="tpu_custom_call" | custom-call | tf_op jit(solution)/shard_map/pallas_call | solution.py:181
  30.2 3.2 %shard_map.86.select_ref = f32[32,128]{1,0:T(8,128)} custom-call(s32[128]{0:T(128)} %owner_ref.1, s32[2]{0:T(128)} %pad_add_fusion.place_ref), custom_call_target="tpu_custom_call" | custom-call | tf_op jit(solution)/shard_map/pallas_call | solution.py:171
  33.5 2.6 %collective-permute-start.2 = (bf16[128,1024]{1,0:T(8,128)(2,1)}, bf16[128,1024]{1,0:T(8,128)(2,1)S(1)}, u32[]{:S(2)}, u32[]{:S(2)}) collective-permute-start(bf16[128,1024]{1,0:T(8,128)(2,1)} %get-tuple-element.70), channel_id=1, source_target_pairs={{0,7},{1,6},{2,5},{3,4},{4,3},{5,2},{6,1},{7,0},{8,15},{9,14},{10,... | collective-permute-start | bytes 786440 | tf_op jit(solution)/shard_map/ppermute | solution.py:163
  38.9 4.5 %collective-permute-done.2.refs_7_ = bf16[128,1024]{1,0:T(8,128)(2,1)S(1)} collective-permute-done((bf16[128,1024]{1,0:T(8,128)(2,1)}, bf16[128,1024]{1,0:T(8,128)(2,1)S(1)}, u32[]{:S(2)}, u32[]{:S(2)}) %collective-permute-start.2) | collective-permute-done | bytes 262176 | tf_op jit(solution)/shard_map/ppermute | solution.py:163
  46.3 14.7 %collective-permute-done.17.refs_4_ = bf16[2,128,768]{2,1,0:T(8,128)(2,1)S(1)} collective-permute-done((bf16[2,128,768]{2,1,0:T(8,128)(2,1)S(1)}, bf16[2,128,768]{2,1,0:T(8,128)(2,1)S(1)}, u32[]{:S(2)}, u32[]{:S(2)}) %collective-permute-start.17) | collective-permute-done | bytes 393248 | tf_op jit(solution)/shard_map/ppermute | solution.py:163
  61.6 4.8 %collective-permute-done.13.refs_4_ = bf16[128,1024]{1,0:T(8,128)(2,1)S(1)} collective-permute-done((bf16[128,1024]{1,0:T(8,128)(2,1)}, bf16[128,1024]{1,0:T(8,128)(2,1)S(1)}, u32[]{:S(2)}, u32[]{:S(2)}) %collective-permute-start.13) | collective-permute-done | bytes 262176 | tf_op jit(solution)/shard_map/ppermute | solution.py:163
  70.5 4.9 %shard_map.88 = (bf16[656,1024]{1,0:T(8,128)(2,1)}, bf16[1024,640]{1,0:T(8,128)(2,1)}, f32[640,128]{1,0:T(8,128)}) custom-call(s32[2]{0:T(128)} %pad_add_fusion.place_ref, bf16[2,128,768]{2,1,0:T(8,128)(2,1)} %copy-done.2, bf16[2,128,768]{2,1,0:T(8,128)(2,1)} %copy-done.4, bf16[2,128,768]{2,1,0:T(8,128)(2,1)} %copy-done.3, bf16[2,128,768]{2,1,0:T(8,128)(2,1)} %copy-done.7, ...), custom_call_target="tpu_custom_call" | custom-call | tf_op jit(solution)/shard_map/pallas_call | solution.py:230
  75.5 8.8 %shard_map.90 = (bf16[128,1024]{1,0:T(8,128)(2,1)}, bf16[128,1024]{1,0:T(8,128)(2,1)}, bf16[128,1024]{1,0:T(8,128)(2,1)}, bf16[128,1024]{1,0:T(8,128)(2,1)}, bf1...) custom-call(s32[2]{0:T(128)} %pad_add_fusion.place_ref, ...), custom_call_target="tpu_custom_call" | custom-call | tf_op jit(solution)/shard_map/pallas_call | solution.py:260
  87.6 1.9 %collective-permute-done.15.refs_5_ = bf16[128,1024]{1,0:T(8,128)(2,1)} collective-permute-done((bf16[128,1024]{1,0:T(8,128)(2,1)}, bf16[128,1024]{1,0:T(8,128)(2,1)}, u32[]{:S(2)}, u32[]{:S(2)}) %collective-permute-start.15) | collective-permute-done | bytes 262176 | tf_op jit(solution)/shard_map/ppermute | solution.py:163
  91.0 4.4 %collective-permute-done.30.refs_2_ = bf16[128,1024]{1,0:T(8,128)(2,1)S(1)} collective-permute-done((bf16[128,1024]{1,0:T(8,128)(2,1)}, bf16[128,1024]{1,0:T(8,128)(2,1)S(1)}, u32[]{:S(2)}, u32[]{:S(2)}) %collective-permute-start.30) | collective-permute-done | bytes 262176 | tf_op jit(solution)/shard_map/ppermute | solution.py:163
  97.0 8.6 %shard_map.89 = (bf16[128,1024]{1,0:T(8,128)(2,1)}, bf16[128,1024]{1,0:T(8,128)(2,1)}, bf16[128,1024]{1,0:T(8,128)(2,1)}, bf16[128,1024]{1,0:T(8,128)(2,1)}, bf1...) custom-call(s32[2]{0:T(128)} %pad_add_fusion.place_ref, ...), custom_call_target="tpu_custom_call" | custom-call | tf_op jit(solution)/shard_map/pallas_call | solution.py:260
  112.9 5.9 %collective-permute-done.25 = f32[32,128]{1,0:T(8,128)S(1)} collective-permute-done((f32[32,128]{1,0:T(8,128)S(1)}, f32[32,128]{1,0:T(8,128)S(1)}, u32[]{:S(2)}, u32[]{:S(2)}) %collective-permute-start.25) | collective-permute-done | bytes 16416 | tf_op jit(solution)/shard_map/ppermute | solution.py:163
  122.6 3.5 %shard_map.91.refs_5_ = bf16[128,16384]{1,0:T(8,128)(2,1)} custom-call(s32[2]{0:T(128)} %pad_add_fusion.place_ref, bf16[128,1024]{1,0:T(8,128)(2,1)} %get-tuple-element.122.refs_0_, bf16[128,1024]{1,0:T(8,128)(2,1)} %copy-done.19, bf16[128,1024]{1,0:T(8,128)(2,1)} %copy-done.18, bf16[128,1024]{1,0:T(8,128)(2,1)} %copy-done.22, bf16[128,1024]{1,0:T(8,128)(2,1)} %copy-done.21, ...), custom_call_target="tpu_custom_call" | custom-call | tf_op jit(solution)/shard_map/pallas_call | solution.py:292
  129.9 1.6 %shard_map.94 = f32[32,128]{1,0:T(8,128)} custom-call(f32[32,128]{1,0:T(8,128)} %shard_map.86.select_ref, f32[128,128]{1,0:T(8,128)} %copy-done.27), custom_call_target="tpu_custom_call" | custom-call | tf_op jit(solution)/shard_map/pallas_call | solution.py:331
  131.5 4.2 %collective-permute-done.39.refs_4_ = bf16[128,1024]{1,0:T(8,128)(2,1)S(1)} collective-permute-done((bf16[128,1024]{1,0:T(8,128)(2,1)S(1)}, bf16[128,1024]{1,0:T(8,128)(2,1)S(1)}, u32[]{:S(2)}, u32[]{:S(2)}) %collective-permute-start.39) | collective-permute-done | bytes 262176 | tf_op jit(solution)/shard_map/ppermute | solution.py:163
  135.7 1.6 %shard_map.92.refs_3_ = bf16[128,16384]{1,0:T(8,128)(2,1)} custom-call(s32[2]{0:T(128)S(1)} %copy-done.1, bf16[128,1024]{1,0:T(8,128)(2,1)S(1)} %copy-done, bf16[128,1024]{1,0:T(8,128)(2,1)S(1)} %collective-permute-done.36.refs_1_, bf16[128,1024]{1,0:T(8,128)(2,1)S(1)} %collective-permute-done.32.refs_2_, ...), custom_call_target="tpu_custom_call", output_to_operand_aliasing={{}: (6, {})} | custom-call | tf_op jit(solution)/shard_map/pallas_call | solution.py:292
  137.4 4.4 %collective-permute-done.33.refs_1_ = bf16[128,1024]{1,0:T(8,128)(2,1)S(1)} collective-permute-done((bf16[128,1024]{1,0:T(8,128)(2,1)S(1)}, bf16[128,1024]{1,0:T(8,128)(2,1)S(1)}, u32[]{:S(2)}, u32[]{:S(2)}) %collective-permute-start.33) | collective-permute-done | bytes 262176 | tf_op jit(solution)/shard_map/ppermute | solution.py:163
  (153 shorter events, 40.6 us)
Async XLA Ops:
  9.0 27.1 %collective-permute-start.16 = (bf16[128,1024]{1,0:T(8,128)(2,1)}, bf16[128,1024]{1,0:T(8,128)(2,1)S(1)}, u32[]{:S(2)}, u32[]{:S(2)}) collective-permute-start(bf16[128,1024]{1,0:T(8,128)(2,1)} %constant_dynamic-slice_fusion.14), channel_id=1, source_target_pairs={{0,3},{1,2},{2,1},{3,0},{4,7},{5,6},{6,5},{7,4},{8,11},{9,10},{10,... | collective-permute-start | bytes 786440 | tf_op jit(solution)/shard_map/ppermute | solution.py:163
  9.0 18.1 %collective-permute-start.11 = (bf16[128,1024]{1,0:T(8,128)(2,1)S(1)}, bf16[128,1024]{1,0:T(8,128)(2,1)S(1)}, u32[]{:S(2)}, u32[]{:S(2)}) collective-permute-start(bf16[128,1024]{1,0:T(8,128)(2,1)S(1)} %constant_dynamic-slice_fusion.15), channel_id=1, source_target_pairs={{0,6},{1,7},{2,4},{3,5},{4,2},{5,3},{6,0},{7,1},{8,14},{9,15},{10,... | collective-permute-start | bytes 786440 | tf_op jit(solution)/shard_map/ppermute | solution.py:163
  11.1 22.4 %collective-permute-start.1 = (bf16[128,1024]{1,0:T(8,128)(2,1)}, bf16[128,1024]{1,0:T(8,128)(2,1)S(1)}, u32[]{:S(2)}, u32[]{:S(2)}) collective-permute-start(bf16[128,1024]{1,0:T(8,128)(2,1)} %constant_dynamic-slice_fusion.16), channel_id=1, source_target_pairs={{0,4},{1,5},{2,6},{3,7},{4,0},{5,1},{6,2},{7,3},{8,12},{9,13},{10,... | collective-permute-start | bytes 786440 | tf_op jit(solution)/shard_map/ppermute | solution.py:163
  20.7 15.9 %collective-permute-start.8 = (bf16[128,1024]{1,0:T(8,128)(2,1)}, bf16[128,1024]{1,0:T(8,128)(2,1)S(1)}, u32[]{:S(2)}, u32[]{:S(2)}) collective-permute-start(bf16[128,1024]{1,0:T(8,128)(2,1)} %get-tuple-element.76), channel_id=1, source_target_pairs={{0,5},{1,4},{2,7},{3,6},{4,1},{5,0},{6,3},{7,2},{8,13},{9,12},{10,... | collective-permute-start | bytes 786440 | tf_op jit(solution)/shard_map/ppermute | solution.py:163
  27.0 17.3 %collective-permute-start.12 = (bf16[2,128,768]{2,1,0:T(8,128)(2,1)S(1)}, bf16[2,128,768]{2,1,0:T(8,128)(2,1)S(1)}, u32[]{:S(2)}, u32[]{:S(2)}) collective-permute-start(bf16[2,128,768]{2,1,0:T(8,128)(2,1)S(1)} %get-tuple-element.80), channel_id=1, source_target_pairs={{0,2},{1,3},{2,0},{3,1},{4,6},{5,7},{6,4},{7,5},{8,10},{9,11},{10,... | collective-permute-start | bytes 1179656 | tf_op jit(solution)/shard_map/ppermute | solution.py:163
  36.1 24.9 %collective-permute-start.17 = (bf16[2,128,768]{2,1,0:T(8,128)(2,1)S(1)}, bf16[2,128,768]{2,1,0:T(8,128)(2,1)S(1)}, u32[]{:S(2)}, u32[]{:S(2)}) collective-permute-start(bf16[2,128,768]{2,1,0:T(8,128)(2,1)S(1)} %get-tuple-element.85), channel_id=1, source_target_pairs={{0,4},{1,5},{2,6},{3,7},{4,0},{5,1},{6,2},{7,3},{8,12},{9,13},{10,... | collective-permute-start | bytes 1179656 | tf_op jit(solution)/shard_map/ppermute | solution.py:163
  37.4 23.6 %collective-permute-start.9 = (bf16[2,128,768]{2,1,0:T(8,128)(2,1)S(1)}, bf16[2,128,768]{2,1,0:T(8,128)(2,1)S(1)}, u32[]{:S(2)}, u32[]{:S(2)}) collective-permute-start(bf16[2,128,768]{2,1,0:T(8,128)(2,1)S(1)} %get-tuple-element.77), channel_id=1, source_target_pairs={{0,6},{1,7},{2,4},{3,5},{4,2},{5,3},{6,0},{7,1},{8,14},{9,15},{10,... | collective-permute-start | bytes 1179656 | tf_op jit(solution)/shard_map/ppermute | solution.py:163
  43.4 18.1 %collective-permute-start.3 = (bf16[128,1024]{1,0:T(8,128)(2,1)}, bf16[128,1024]{1,0:T(8,128)(2,1)S(1)}, u32[]{:S(2)}, u32[]{:S(2)}) collective-permute-start(bf16[128,1024]{1,0:T(8,128)(2,1)} %get-tuple-element.71), channel_id=1, source_target_pairs={{0,2},{1,3},{2,0},{3,1},{4,6},{5,7},{6,4},{7,5},{8,10},{9,11},{10,... | collective-permute-start | bytes 786440 | tf_op jit(solution)/shard_map/ppermute | solution.py:163
  44.3 22.0 %collective-permute-start.13 = (bf16[128,1024]{1,0:T(8,128)(2,1)}, bf16[128,1024]{1,0:T(8,128)(2,1)S(1)}, u32[]{:S(2)}, u32[]{:S(2)}) collective-permute-start(bf16[128,1024]{1,0:T(8,128)(2,1)} %get-tuple-element.81), channel_id=1, source_target_pairs={{0,4},{1,5},{2,6},{3,7},{4,0},{5,1},{6,2},{7,3},{8,12},{9,13},{10,... | collective-permute-start | bytes 786440 | tf_op jit(solution)/shard_map/ppermute | solution.py:163
  45.9 21.0 %collective-permute-start.14 = (bf16[2,128,768]{2,1,0:T(8,128)(2,1)S(1)}, bf16[2,128,768]{2,1,0:T(8,128)(2,1)S(1)}, u32[]{:S(2)}, u32[]{:S(2)}) collective-permute-start(bf16[2,128,768]{2,1,0:T(8,128)(2,1)S(1)} %collective-permute-done.12.refs_2_), channel_id=1, source_target_pairs={{0,1},{1,0},{2,3},{3,2},{4,5},{5,4},{6,7},{7,6},{8,9},{9,8},{10,11... | collective-permute-start | bytes 1179656 | tf_op jit(solution)/shard_map/ppermute | solution.py:162
  61.5 14.0 %collective-permute-start.22 = (bf16[128,1024]{1,0:T(8,128)(2,1)}, bf16[128,1024]{1,0:T(8,128)(2,1)}, u32[]{:S(2)}, u32[]{:S(2)}) collective-permute-start(bf16[128,1024]{1,0:T(8,128)(2,1)} %get-tuple-element.128), channel_id=1, source_target_pairs={{0,1},{1,0},{2,3},{3,2},{4,5},{5,4},{6,7},{7,6},{8,9},{9,8},{10,11... | collective-permute-start | bytes 786440 | tf_op jit(solution)/shard_map/ppermute | solution.py:162
  66.3 18.0 %collective-permute-start.10 = (bf16[128,1024]{1,0:T(8,128)(2,1)}, bf16[128,1024]{1,0:T(8,128)(2,1)}, u32[]{:S(2)}, u32[]{:S(2)}) collective-permute-start(bf16[128,1024]{1,0:T(8,128)(2,1)} %get-tuple-element.78), channel_id=1, source_target_pairs={{0,3},{1,2},{2,1},{3,0},{4,7},{5,6},{6,5},{7,4},{8,11},{9,10},{10,... | collective-permute-start | bytes 786440 | tf_op jit(solution)/shard_map/ppermute | solution.py:163
  66.9 18.7 %collective-permute-start.18 = (bf16[128,1024]{1,0:T(8,128)(2,1)}, bf16[128,1024]{1,0:T(8,128)(2,1)}, u32[]{:S(2)}, u32[]{:S(2)}) collective-permute-start(bf16[128,1024]{1,0:T(8,128)(2,1)} %get-tuple-element.86), channel_id=1, source_target_pairs={{0,6},{1,7},{2,4},{3,5},{4,2},{5,3},{6,0},{7,1},{8,14},{9,15},{10,... | collective-permute-start | bytes 786440 | tf_op jit(solution)/shard_map/ppermute | solution.py:163
  68.5 18.4 %collective-permute-start.19 = (bf16[128,1024]{1,0:T(8,128)(2,1)}, bf16[128,1024]{1,0:T(8,128)(2,1)}, u32[]{:S(2)}, u32[]{:S(2)}) collective-permute-start(bf16[128,1024]{1,0:T(8,128)(2,1)} %get-tuple-element.87), channel_id=1, source_target_pairs={{0,7},{1,6},{2,5},{3,4},{4,3},{5,2},{6,1},{7,0},{8,15},{9,14},{10,... | collective-permute-start | bytes 786440 | tf_op jit(solution)/shard_map/ppermute | solution.py:163
  69.6 19.8 %collective-permute-start.15 = (bf16[128,1024]{1,0:T(8,128)(2,1)}, bf16[128,1024]{1,0:T(8,128)(2,1)}, u32[]{:S(2)}, u32[]{:S(2)}) collective-permute-start(bf16[128,1024]{1,0:T(8,128)(2,1)} %get-tuple-element.83), channel_id=1, source_target_pairs={{0,5},{1,4},{2,7},{3,6},{4,1},{5,0},{6,3},{7,2},{8,13},{9,12},{10,... | collective-permute-start | bytes 786440 | tf_op jit(solution)/shard_map/ppermute | solution.py:163
  85.6 21.8 %collective-permute-start.26 = (bf16[128,1024]{1,0:T(8,128)(2,1)}, bf16[128,1024]{1,0:T(8,128)(2,1)S(1)}, u32[]{:S(2)}, u32[]{:S(2)}) collective-permute-start(bf16[128,1024]{1,0:T(8,128)(2,1)} %get-tuple-element.101), channel_id=1, source_target_pairs={{0,2},{1,3},{2,0},{3,1},{4,6},{5,7},{6,4},{7,5},{8,10},{9,11},{10,... | collective-permute-start | bytes 786440 | tf_op jit(solution)/shard_map/ppermute | solution.py:163
  86.8 23.0 %collective-permute-start.35 = (bf16[128,1024]{1,0:T(8,128)(2,1)}, bf16[128,1024]{1,0:T(8,128)(2,1)S(1)}, u32[]{:S(2)}, u32[]{:S(2)}) collective-permute-start(bf16[128,1024]{1,0:T(8,128)(2,1)} %get-tuple-element.117), channel_id=1, source_target_pairs={{0,3},{1,2},{2,1},{3,0},{4,7},{5,6},{6,5},{7,4},{8,11},{9,10},{10,... | collective-permute-start | bytes 786440 | tf_op jit(solution)/shard_map/ppermute | solution.py:163
  89.5 21.3 %collective-permute-start.24 = (bf16[128,1024]{1,0:T(8,128)(2,1)}, bf16[128,1024]{1,0:T(8,128)(2,1)S(1)}, u32[]{:S(2)}, u32[]{:S(2)}) collective-permute-start(bf16[128,1024]{1,0:T(8,128)(2,1)} %get-tuple-element.97), channel_id=1, source_target_pairs={{0,6},{1,7},{2,4},{3,5},{4,2},{5,3},{6,0},{7,1},{8,14},{9,15},{10,... | collective-permute-start | bytes 786440 | tf_op jit(solution)/shard_map/ppermute | solution.py:163
  95.4 16.5 %collective-permute-start.31 = (bf16[128,1024]{1,0:T(8,128)(2,1)}, bf16[128,1024]{1,0:T(8,128)(2,1)S(1)}, u32[]{:S(2)}, u32[]{:S(2)}) collective-permute-start(bf16[128,1024]{1,0:T(8,128)(2,1)} %get-tuple-element.110), channel_id=1, source_target_pairs={{0,7},{1,6},{2,5},{3,4},{4,3},{5,2},{6,1},{7,0},{8,15},{9,14},{10,... | collective-permute-start | bytes 786440 | tf_op jit(solution)/shard_map/ppermute | solution.py:163
  107.4 13.8 %collective-permute-start.38 = (bf16[128,1024]{1,0:T(8,128)(2,1)S(1)}, bf16[128,1024]{1,0:T(8,128)(2,1)S(1)}, u32[]{:S(2)}, u32[]{:S(2)}) collective-permute-start(bf16[128,1024]{1,0:T(8,128)(2,1)S(1)} %copy-done.31), channel_id=1, source_target_pairs={{0,1},{1,0},{2,3},{3,2},{4,5},{5,4},{6,7},{7,6},{8,9},{9,8},{10,11... | collective-permute-start | bytes 786440 | tf_op jit(solution)/shard_map/ppermute | solution.py:162
  109.8 16.4 %collective-permute-start.36 = (bf16[128,1024]{1,0:T(8,128)(2,1)}, bf16[128,1024]{1,0:T(8,128)(2,1)S(1)}, u32[]{:S(2)}, u32[]{:S(2)}) collective-permute-start(bf16[128,1024]{1,0:T(8,128)(2,1)} %get-tuple-element.118), channel_id=1, source_target_pairs={{0,2},{1,3},{2,0},{3,1},{4,6},{5,7},{6,4},{7,5},{8,10},{9,11},{10,... | collective-permute-start | bytes 786440 | tf_op jit(solution)/shard_map/ppermute | solution.py:163
  111.8 16.3 %collective-permute-start.32 = (bf16[128,1024]{1,0:T(8,128)(2,1)}, bf16[128,1024]{1,0:T(8,128)(2,1)S(1)}, u32[]{:S(2)}, u32[]{:S(2)}) collective-permute-start(bf16[128,1024]{1,0:T(8,128)(2,1)} %get-tuple-element.111), channel_id=1, source_target_pairs={{0,4},{1,5},{2,6},{3,7},{4,0},{5,1},{6,2},{7,3},{8,12},{9,13},{10,... | collective-permute-start | bytes 786440 | tf_op jit(solution)/shard_map/ppermute | solution.py:163
  121.2 16.2 %collective-permute-start.34 = (bf16[128,1024]{1,0:T(8,128)(2,1)}, bf16[128,1024]{1,0:T(8,128)(2,1)S(1)}, u32[]{:S(2)}, u32[]{:S(2)}) collective-permute-start(bf16[128,1024]{1,0:T(8,128)(2,1)} %get-tuple-element.113), channel_id=1, source_target_pairs={{0,1},{1,0},{2,3},{3,2},{4,5},{5,4},{6,7},{7,6},{8,9},{9,8},{10,11... | collective-permute-start | bytes 786440 | tf_op jit(solution)/shard_map/ppermute | solution.py:162
  128.1 13.6 %collective-permute-start.33 = (bf16[128,1024]{1,0:T(8,128)(2,1)S(1)}, bf16[128,1024]{1,0:T(8,128)(2,1)S(1)}, u32[]{:S(2)}, u32[]{:S(2)}) collective-permute-start(bf16[128,1024]{1,0:T(8,128)(2,1)S(1)} %copy-done.29), channel_id=1, source_target_pairs={{0,7},{1,6},{2,5},{3,4},{4,3},{5,2},{6,1},{7,0},{8,15},{9,14},{10,... | collective-permute-start | bytes 786440 | tf_op jit(solution)/shard_map/ppermute | solution.py:163
  (50 other events, 646.2 us)
